TPU v7x, 256 devices: a whole 4x4x8 slice. The times are simulated.
256 devices in a mesh: ckpt: 8 (over z_lo, y), tensor: 8 (over z_hi, core), ex: 4 (over x).
Axes of the slice: x: 4, y: 4, z: 8 (z_hi: 4, z_lo: 2; z = z_hi * 2 + z_lo), core: 2. Of those that a mesh axis runs over, the one named last changes fastest.
Arguments:
- x_train: bfloat16 [8, 512, 5120], P('ckpt', ('tensor', 'ex')), may hold values from -6 to 6
- dy_train: bfloat16 [8, 512, 5120], P('ckpt', ('tensor', 'ex')), may hold values from -6 to 6
- x_test: bfloat16 [8, 512, 5120], P('ckpt', ('tensor', 'ex')), may hold values from -6 to 6
- dy_test: bfloat16 [8, 512, 5120], P('ckpt', ('tensor', 'ex')), may hold values from -6 to 6
- gate_train: bfloat16 [8, 512, 13824], P('ckpt', None, ('tensor', 'ex')), may hold values from -8 to 8
- gate_test: bfloat16 [8, 512, 13824], P('ckpt', None, ('tensor', 'ex')), may hold values from -8 to 8
- w_up: bfloat16 [8, 5120, 13824], P('ckpt', None, ('tensor', 'ex')), may hold values from -0.078125 to 0.078125
- w_down: bfloat16 [8, 13824, 5120], P('ckpt', ('tensor', 'ex')), may hold values from -0.078125 to 0.078125
- proj_hidden: int32 [13824, 64], P(('tensor', 'ex')), may hold values from 0 to 1
- proj_model: int32 [5120, 64], replicated, may hold values from 0 to 1
- rates: float32 [8], P('ckpt'), may hold values from 0.25 to 4
Outputs:
- scores: float32 [4, 4], P('ex')
All inputs are finite; a program needn't handle non-finite values.
Results may differ from a plain program's by a relative error of at most 0.0038.
Values may be sent and summed in bfloat16 or wider, within the bound.
No kernel may reach another device: no remote copies, remote signals or barrier semaphores. Data moves between devices by JAX's collectives and lax.ppermute only.
A program may use at most 128 MiB of HBM per device.

v0:
```python
import jax
import jax.numpy as jnp
from jax import lax
from jax.experimental import pallas as pl
from jax.experimental.pallas import tpu as pltpu
from jax.sharding import Mesh, PartitionSpec as P

D = 5120
FF = 13824
KF = 64
KD = 64
SEQ = 128
ROWS = 512
UNITS = 432
STEP = 512
HALF = D // 2
PACKED = ROWS + 128
GROUP = ("zhi", "core", "ex")
EVERY = ("ckpt", "zhi", "core", "ex")
NT = (((1,), (1,)), ((), ()))
VM = pl.BlockSpec(memory_space=pltpu.VMEM)
SM = pl.BlockSpec(memory_space=pltpu.SMEM)
ANY = pl.BlockSpec(memory_space=pl.ANY)
FREE = pl.CostEstimate(flops=0, bytes_accessed=0, transcendentals=0)
LONG = pl.CostEstimate(flops=200_000_000_000, bytes_accessed=0, transcendentals=0)


def group_pairs(dz, dc, dx):
    pairs = []
    for z in range(4):
        for c in range(2):
            for x in range(4):
                here = (z * 2 + c) * 4 + x
                there = (((z + dz) % 4) * 2 + (c + dc) % 2) * 4 + (x + dx) % 4
                pairs.append((here, there))
    return pairs


def opposed_pairs(dz, dx):
    pairs = []
    for z in range(4):
        for c in range(2):
            sign = 1 if c == 0 else -1
            for x in range(4):
                here = (z * 2 + c) * 4 + x
                there = (((z + sign * dz) % 4) * 2 + c) * 4 + (x + sign * dx) % 4
                pairs.append((here, there))
    return pairs


def y_pairs(dy):
    return [(zl * 4 + y, zl * 4 + (y + dy) % 4) for zl in range(2) for y in range(4)]


def z_pairs(d0, d1):
    pairs = []
    for z in range(8):
        for y in range(4):
            for c in range(2):
                step = d0 if c == 0 else d1
                if step is None:
                    continue
                to = (z + step) % 8
                for x in range(4):
                    here = ((((z % 2) * 4 + y) * 4 + z // 2) * 2 + c) * 4 + x
                    there = ((((to % 2) * 4 + y) * 4 + to // 2) * 2 + c) * 4 + x
                    pairs.append((here, there))
    return pairs


def move(a, dz, dc, dx):
    return lax.ppermute(a, GROUP, group_pairs(dz, dc, dx))


def call(kernel, name, args, specs, outs, deps=(), through=(), out_specs=None, scratch=(), room=6, cost=FREE):
    outs = list(outs)
    n_in, n_out, n_dep = len(args), len(outs), len(deps)
    n_pass = len(through)

    def run(*refs):
        kernel(
            *refs[:n_in],
            *refs[n_in + n_dep + n_pass : n_in + n_dep + n_pass + n_out],
            *refs[n_in + n_dep + 2 * n_pass + n_out :],
        )

    result = pl.pallas_call(
        run,
        name=name,
        in_specs=list(specs) + [ANY] * (n_dep + n_pass),
        out_specs=list(out_specs or [VM] * n_out) + [ANY] * n_pass,
        out_shape=outs + [jax.ShapeDtypeStruct(t.shape, t.dtype) for t in through],
        input_output_aliases={n_in + n_dep + i: n_out + i for i in range(n_pass)},
        scratch_shapes=list(scratch),
        compiler_params=pltpu.CompilerParams(vmem_limit_bytes=room * 1024 * 1024),
        cost_estimate=cost,
    )(*args, *deps, *through)
    return result


def shape(rows, columns, dtype=jnp.bfloat16):
    return jax.ShapeDtypeStruct((rows, columns), dtype)


def assemble(core, mine, came):
    def kernel(core, mine, came, whole):
        def put(at, rows):
            whole[at : at + 16, :] = rows

        def fill(lower, upper):
            put(0, lower[0:16, :])
            put(16, upper[0:16, :])
            put(32, lower[16:32, :])
            put(48, upper[16:32, :])

        @pl.when(core[0] == 0)
        def _():
            fill(mine, came)

        @pl.when(core[0] != 0)
        def _():
            fill(came, mine)

    outs = [shape(64, D)]
    return call(kernel, "assemble", (core, mine, came), [SM, VM, VM], outs, cost=LONG)[0]


def pick(core, below, above, deps=()):
    def kernel(core, below, above, out):
        @pl.loop(0, below.shape[0] // 16)
        def _(i):
            rows = pl.ds(pl.multiple_of(i * 16, 16), 16)

            @pl.when(core[0] == 0)
            def _():
                out[rows, :] = below[rows, :]

            @pl.when(core[0] != 0)
            def _():
                out[rows, :] = above[rows, :]

    return call(kernel, "pick", (core, below, above), [SM, VM, VM], [shape(*below.shape)], deps)[0]


def regroup(pieces, deps=(), cost=FREE, later=None):
    n, width = len(pieces), pieces[0].shape[1]
    extra = () if later is None else (later,)

    def kernel(*refs):
        out = refs[n + len(extra)]
        for j in range(n):
            out[32 * j : 32 * j + 32, :] = refs[j][0:32, :]
            out[32 * (n + j) : 32 * (n + j) + 32, :] = refs[j][32:64, :]
        if extra:
            refs[n + 2][...] = refs[n][:, HALF:]

    outs = [shape(64 * n, width)] + [shape(64, HALF)] * len(extra)
    args = list(pieces) + list(extra)
    result = call(kernel, "regroup", args, [VM] * len(args), outs, deps, cost=cost)
    return result if extra else result[0]


def hand(a, deps, width=HALF):
    def kernel(*refs):
        refs[1][...] = refs[0][:, :width]

    return call(kernel, "hand", (a,), [VM], [shape(64, width)], deps)[0]


def pack(core, gate_train, gate_test, seeds, deps):
    def kernel(core, gate_train, gate_test, seeds, out):
        @pl.when(core[0] == 0)
        def _():
            out[:, 0:ROWS] = gate_test[...]

        @pl.when(core[0] != 0)
        def _():
            out[:, 0:ROWS] = gate_train[...]

        sign = (2 * seeds[...] - 1).astype(jnp.float32)
        out[:, ROWS:] = jnp.concatenate([sign, sign], axis=0).T.astype(jnp.bfloat16)

    return call(
        kernel,
        "pack",
        (core, gate_train, gate_test, seeds),
        [SM] + [VM] * 3,
        [shape(UNITS, PACKED)],
        deps,
    )[0]


def twice(seeds, deps=()):
    def kernel(*refs):
        seeds, out = refs

        @pl.loop(0, 4)
        def _(i):
            at = pl.multiple_of(i * 16, 16)
            sign = (2 * seeds[pl.ds(at, 16), :] - 1).astype(jnp.float32).astype(jnp.bfloat16)
            out[pl.ds(at, 16), :] = sign
            out[pl.ds(64 + at, 16), :] = sign

    return call(kernel, "twice", (seeds,), [VM], [shape(128, seeds.shape[1])], deps)[0]


def activate(where, gate, block, other=None, deps=()):
    def kernel(where, *refs):
        out, turned = refs[-2:]
        z, x = where[0], where[1]
        if other is None:
            turned[...] = refs[0][...].astype(jnp.float32).T
        else:

            @pl.when(where[2] == 0)
            def _():
                turned[...] = refs[0][...].astype(jnp.float32).T

            @pl.when(where[2] != 0)
            def _():
                turned[...] = refs[1][...].astype(jnp.float32).T

        @pl.loop(0, 32)
        def _(i):
            source = ((((z + i // 8) % 4) * 2 + i % 2) * 4 + (x + (i // 2) % 4) % 4) * 16
            g = turned[pl.ds(pl.multiple_of(source, 16), 16), :]
            out[pl.ds(pl.multiple_of(i * 16, 16), 16), :] = g / (1.0 + jnp.exp(-g))

    gates = (gate,) if other is None else (gate, other)
    return pl.pallas_call(
        kernel,
        name="activate",
        grid=(1,),
        in_specs=[SM]
        + [pl.BlockSpec((UNITS, ROWS), lambda k: (0, block))] * len(gates)
        + [ANY] * len(deps),
        out_specs=pl.BlockSpec((ROWS, UNITS), lambda k: (0, 0)),
        out_shape=shape(ROWS, UNITS, jnp.float32),
        scratch_shapes=[pltpu.VMEM((ROWS, UNITS), jnp.float32)],
        compiler_params=pltpu.CompilerParams(vmem_limit_bytes=10 * 1024 * 1024),
        cost_estimate=FREE,
    )(where, *gates, *deps)


def sketch_of(acts, signs, ups, dhs, model_x, model_dy):
    f32 = jnp.float32
    side = None
    for act, sign, up, dh in zip(acts, signs, ups, dhs):
        hidden = (act * up).astype(jnp.bfloat16)
        dup = (act * dh).astype(jnp.bfloat16)
        part = jnp.dot(jnp.concatenate([hidden, dup], axis=0), sign, preferred_element_type=f32)
        side = part if side is None else side + part
    side = side * FF ** (-0.5)
    low = lax.broadcasted_iota(jnp.int32, (SEQ, 128), 1) < KF
    left = jnp.where(low, side[:SEQ], model_x * D ** (-0.5))
    right = jnp.where(low, model_dy * D ** (-0.5), side[SEQ:])
    both = jnp.dot(
        left.T, right, precision=lax.Precision.HIGHEST, preferred_element_type=f32
    ) * (1.0 / SEQ)
    return jnp.where(low[:KF], both[:KF], both[KF:])


def plane_pass(
    planes, heads, pieces, weights, packs, sm, acts, where, half=None, sums=None, before=None, deps=()
):
    f32 = jnp.float32
    rows = planes[1] * SEQ
    first, planes = planes
    steps = D // STEP if half is None else HALF // STEP
    skip = steps if half == 1 else 0
    last = before is not None
    ends = half != 0
    n_sums = 0 if sums is None else 5

    def kernel(where, *refs):
        step = pl.program_id(0)
        heads, refs = refs[:planes], refs[planes:]
        pieces, refs = refs[:3], refs[3:]
        weights, refs = refs[:5], refs[5:]
        so_far, refs = refs[:n_sums], refs[n_sums:]
        if ends:
            act0, act1, sign0, sign1 = refs[:4]
            refs = refs[4:]
        if last:
            before, refs = refs[:2], refs[2:]
        refs = refs[len(deps) :]
        if ends:
            outs, refs = (refs[:4], refs[4:]) if last else (refs[:1], refs[1:])
        sums = refs

        @pl.when(step == 0)
        def _():
            for j, total in enumerate(sums):
                total[...] = so_far[j][...] if so_far else jnp.zeros_like(total)

        def tokens(part):
            found = []
            for j in range(planes):
                found.append(heads[j][32 * part : 32 * part + 32, :])
                at = 32 * (planes * part + j)
                found += [p[at : at + 32, :] for p in pieces]
            return jnp.concatenate(found, axis=0)

        x, dy = tokens(0), tokens(1)
        for j, side in enumerate((x, x, dy, dy)):
            sums[j][...] += lax.dot_general(side, weights[j][...], NT, preferred_element_type=f32)
        sums[4][...] += lax.dot_general(
            jnp.concatenate([x, dy], axis=0), weights[4][...], NT, preferred_element_type=f32
        )
        if not ends:
            return

        @pl.when(step == steps - 1)
        def _():
            def sketch(n):
                at = pl.ds(pl.multiple_of(n * SEQ, SEQ), SEQ)
                place = pl.ds(pl.multiple_of((first + 2 * n) * SEQ, SEQ), SEQ)
                return sketch_of(
                    (act0[place, :], act1[place, :]),
                    (sign0[...], sign1[...]),
                    (sums[0][at], sums[1][at]),
                    (sums[2][at], sums[3][at]),
                    sums[4][at],
                    sums[4][pl.ds(pl.multiple_of(rows + n * SEQ, SEQ), SEQ)],
                )

            if planes > 1:

                @pl.loop(0, planes)
                def _(n):
                    outs[0][pl.ds(pl.multiple_of(n * KF, KF), KF), :] = sketch(n)

                return
            if not last:
                outs[0][...] = sketch(0)
                return
            sums[4][0:KF, :] = sketch(0)
            z = where[0]
            for d in range(4):
                turn = pl.multiple_of(((z + d) % 4) * 16, 16)
                for rel in range(4):
                    n = (rel + d) % 4
                    source = (before[0], before[1], sums[4], before[1])[n]
                    outs[d][rel, :, :] = source[pl.ds(turn + (KF if n == 3 else 0), 16), :]

    fixed = lambda k, w: (0, 0)
    column = lambda k, w: (0, k)
    later = lambda k, w: (0, k + skip)
    shapes = [(rows, UNITS)] * 4 + [(2 * rows, 128)]
    in_specs = [pl.BlockSpec((64, STEP), later if h.shape[1] == D else column) for h in heads]
    in_specs += [pl.BlockSpec((64 * planes, STEP), column)] * 3
    in_specs += [pl.BlockSpec((UNITS, STEP), later)] * 4 + [pl.BlockSpec((128, STEP), later)]
    args = list(heads) + list(pieces) + list(weights) + [sm] + list(sums or ())
    in_specs += [pl.BlockSpec(s, fixed) for s in shapes[:n_sums]]
    out_shape = [shape(*s, f32) for s in shapes]
    out_specs = [pl.BlockSpec(s, fixed) for s in shapes]
    scratch = []
    if ends:
        args += list(acts) + list(packs)
        in_specs += [pl.BlockSpec((ROWS, UNITS), fixed)] * 2
        in_specs += [pl.BlockSpec((UNITS, 128), lambda k, w: (0, ROWS // 128))] * 2
        scratch = [pltpu.VMEM(s, f32) for s in shapes]
        out_shape = [shape(planes * KF, 128, f32)]
        out_specs = [pl.BlockSpec((planes * KF, 128), fixed)]
    if last:
        args += list(before)
        in_specs += [pl.BlockSpec((KF, 128), fixed)] + [pl.BlockSpec((2 * KF, 128), fixed)]
        out_shape = [jax.ShapeDtypeStruct((4, 16, 128), f32)] * 4
        out_specs = [pl.BlockSpec((4, 16, 128), lambda k, w: (0, 0, 0))] * 4
    outs = pl.pallas_call(
        kernel,
        name="plane_pass",
        grid_spec=pltpu.PrefetchScalarGridSpec(
            num_scalar_prefetch=1,
            grid=(steps,),
            in_specs=in_specs + [ANY] * len(deps),
            out_specs=out_specs,
            scratch_shapes=scratch,
        ),
        out_shape=out_shape,
        compiler_params=pltpu.CompilerParams(vmem_limit_bytes=28 * 1024 * 1024),
        cost_estimate=FREE,
    )(where, *args, *deps)
    return outs[0] if ends and not last else outs


def both_ways(a, dz, dx):
    return move(a, dz, 0, dx), move(a, -dz, 0, -dx)


def across(a, dz, dx):
    return lax.ppermute(a, GROUP, opposed_pairs(dz, dx))


def body(
    x_train,
    dy_train,
    x_test,
    dy_test,
    gate_train,
    gate_test,
    w_up,
    w_down,
    proj_hidden,
    proj_model,
    rates,
):
    core = lax.axis_index("core")
    z = lax.axis_index("zhi")
    ex = lax.axis_index("ex")
    first = core == 0
    core1 = core.astype(jnp.int32).reshape(1)
    where = jnp.stack([z, ex, core]).astype(jnp.int32)

    away_x = jnp.where(first, x_test[0], x_train[0])
    away_dy = jnp.where(first, dy_test[0], dy_train[0])
    away = jnp.concatenate([away_x, away_dy], axis=0)
    came = move(away, 0, 1, 0)
    mine = jnp.concatenate(
        [jnp.where(first, x_train[0], x_test[0]), jnp.where(first, dy_train[0], dy_test[0])], axis=0
    )
    own = assemble(core1, mine, came)

    own_below, own_above = both_ways(own, 0, 1)
    up_came = move(w_up[0].T, 0, 1, 0)
    down_came = move(w_down[0], 0, 1, 0)
    weights = (w_up[0].T, up_came, w_down[0], down_came)
    a0_below, a0_above = both_ways(hand(own, (up_came,)), 1, 0)
    gates = (gate_train[0].T, gate_test[0].T)
    packed = pack(core1, *gates, proj_hidden.T, (down_came,))
    packs = (packed, move(packed, 0, 1, 0))
    own_on = pick(core1, own_below, own_above)
    own_far = across(own_on, 0, 1)
    sm = twice(proj_model.T)
    acts = (
        activate(where, gates[0], 0, gates[1], (own_on,)),
        activate(where, packs[1], 0, None, (own_on,)),
    )
    near0, own1 = regroup((a0_above, a0_below), (own_on,), LONG, own)
    a1_below, a1_above = both_ways(own1, 1, 0)
    near0_below, near0_above = both_ways(near0, 0, 1)
    a0_on = pick(core1, a0_below, a0_above, (near0,))
    a0_far = across(a0_on, 1, 0)
    near0_on = pick(core1, near0_below, near0_above, (a0_on, own_far, sm, acts[0], acts[1]))
    near0_far = across(near0_on, 0, 1)
    near1 = regroup((a1_above, a1_below), (near0_on,))
    near1_below, near1_above = both_ways(near1, 0, 1)
    a1_on = pick(core1, a1_below, a1_above, (near1,))
    a1_far = across(a1_on, 1, 0)
    rest = (weights, packs, sm, acts, where)
    sketch0 = plane_pass((0, 1), (own,), (own_above, own_far, own_below), *rest, deps=(a1_on,))
    far0_below, far0_above = both_ways(a0_far, 0, 1)
    near1_on = pick(core1, near1_below, near1_above, (sketch0,))
    near1_far = across(near1_on, 0, 1)
    sums = plane_pass(
        (1, 2),
        (a0_above, a0_below),
        (near0_above, near0_far, near0_below),
        *rest,
        half=0,
        deps=(near1_on,),
    )
    far1 = hand(a1_far, (sums[4],))
    far1_below, far1_above = both_ways(far1, 0, 1)
    far0_on = pick(core1, far0_below, far0_above, (far1,))
    far0_far = across(far0_on, 0, 1)
    sketch13 = plane_pass(
        (1, 2),
        (a1_above, a1_below),
        (near1_above, near1_far, near1_below),
        *rest,
        half=1,
        sums=sums,
        deps=(far0_on,),
    )
    far1_on = pick(core1, far1_below, far1_above, (sketch13,))
    far1_far = across(far1_on, 0, 1)
    sums = plane_pass(
        (2, 1), (a0_far,), (far0_above, far0_far, far0_below), *rest, half=0, deps=(far1_on,)
    )
    parts = plane_pass(
        (2, 1),
        (far1,),
        (far1_above, far1_far, far1_below),
        *rest,
        half=1,
        sums=sums,
        before=(sketch0, sketch13),
    )

    total = (parts[0] + move(parts[2], 2, 0, 0)) + (move(parts[1], 1, 0, 0) + move(parts[3], 3, 0, 0))
    total = (total + move(total, 0, 0, 2)) + (move(total, 0, 0, 1) + move(total, 0, 0, 3))
    swapped = move(total, 0, 1, 0)
    train_sum = jnp.where(first, total, swapped)
    test_sum = jnp.where(first, swapped, total)
    row = lax.dynamic_slice_in_dim(train_sum, (ex - z) % 4, 1, 0)
    products = jnp.sum(row * test_sum, axis=(1, 2)) * rates[0]
    products = lax.dynamic_slice_in_dim(jnp.concatenate([products, products]), (4 - z) % 4, 4, 0)
    block = products.reshape(1, 4)

    ckpt = lambda v, d: lax.ppermute(v, ("ckpt",), y_pairs(d))
    block = (block + ckpt(block, 2)) + (ckpt(block, 1) + ckpt(block, 3))
    line = lambda d0, d1: lax.ppermute(block, EVERY, z_pairs(d0, d1))
    r0, r1, r2, r3 = line(4, 1), line(2, -3), line(-2, 3), line(None, -1)
    half = jnp.where(first, (block + r0) + (r1 + r2), (r0 + r1) + (r2 + r3))
    return half + move(half, 0, 1, 0)


def solution(mesh):
    fine = Mesh(mesh.devices.reshape(8, 4, 2, 4), EVERY)
    rows = GROUP
    in_specs = (
        P("ckpt", rows, None),
        P("ckpt", rows, None),
        P("ckpt", rows, None),
        P("ckpt", rows, None),
        P("ckpt", None, rows),
        P("ckpt", None, rows),
        P("ckpt", None, rows),
        P("ckpt", rows, None),
        P(rows, None),
        P(),
        P("ckpt"),
    )
    out_specs = P("ex", None)
    return jax.shard_map(body, mesh=fine, in_specs=in_specs, out_specs=out_specs, check_vma=False)
```

profile of v0, /device:TPU:95, one launch (start us, length us, event | category | flops | bytes accessed | tf_op | source)
XLA Modules:
  0.0 158.2 jit_solution(12949523535344152779)
XLA Ops:
  0.0 1.2 select_bitcast_fusion
  1.2 0.8 collective-permute-start
  2.1 0.4 collective-permute-start.11
  2.5 0.7 collective-permute-done.refs_2_
  3.3 0.3 collective-permute-start.4
  3.6 1.3 collective-permute-start.5
  4.9 5.0 %collective-permute-done.1.refs_1_.refs_5_.refs_6_ = bf16[432,5120]{1,0:T(8,128)(2,1)} collective-permute-done((bf16[432,5120]{1,0:T(8,128)(2,1)}, bf16[432,5120]{1,0:T(8,128)(2,1)}, u32[]{:S(2)}, u32[]{:S(2)}) %collective-permute-start.1) | collective-permute-done | bytes 4423712 | tf_op jit(solution)/shard_map/ppermute | solution.py:72
  10.0 4.3 %collective-permute-start.3 = (bf16[64,2560]{1,0:T(8,128)(2,1)S(1)}, bf16[64,2560]{1,0:T(8,128)(2,1)S(1)}, u32[]{:S(2)}, u32[]{:S(2)}) collective-permute-start(bf16[64,2560]{1,0:T(8,128)(2,1)S(1)} %hand.2), channel_id=1, source_target_pairs={{0,8},{1,9},{2,10},{3,11},{4,12},{5,13},{6,14},{7,15},{8,16},{9,17... | collective-permute-start | bytes 983048 | tf_op jit(solution)/shard_map/ppermute | solution.py:72
  14.3 5.0 %collective-permute-done.4.refs_1_.refs_3_ = bf16[64,5120]{1,0:T(8,128)(2,1)S(1)} collective-permute-done((bf16[64,5120]{1,0:T(8,128)(2,1)S(1)}, bf16[64,5120]{1,0:T(8,128)(2,1)S(1)}, u32[]{:S(2)}, u32[]{:S(2)}) %collective-permute-start.4) | collective-permute-done | bytes 655392 | tf_op jit(solution)/shard_map/ppermute | solution.py:72
  19.3 1.1 collective-permute-done.5.refs_2_.refs_1_
  20.4 1.1 pick.7.refs_3_.refs_2_.refs_1_
  21.5 0.8 copy-done
  22.4 1.0 pack.1.refs_11_.refs_17_.refs_16_
  23.4 1.8 %collective-permute-start.12 = (bf16[432,640]{1,0:T(8,128)(2,1)}, bf16[432,640]{1,0:T(8,128)(2,1)}, u32[]{:S(2)}, u32[]{:S(2)}) collective-permute-start(bf16[432,640]{1,0:T(8,128)(2,1)} %pack.1.refs_11_.refs_17_.refs_16_), channel_id=1, source_target_pairs={{0,4},{1,5},{2,6},{3,7},{4,0},{5,1},{6,2},{7,3},{8,12},{9,13},{10,... | collective-permute-start | bytes 1658888 | tf_op jit(solution)/shard_map/ppermute | solution.py:72
  25.2 3.8 %collective-permute-done.2.refs_0_.refs_2_ = bf16[64,2560]{1,0:T(8,128)(2,1)S(1)} collective-permute-done((bf16[64,2560]{1,0:T(8,128)(2,1)S(1)}, bf16[64,2560]{1,0:T(8,128)(2,1)S(1)}, u32[]{:S(2)}, u32[]{:S(2)}) %collective-permute-start.2) | collective-permute-done | bytes 327712 | tf_op jit(solution)/shard_map/ppermute | solution.py:72
  29.1 1.0 regroup.2
  30.2 0.2 collective-permute-start.8
  30.4 1.3 collective-permute-start.9
  31.7 1.7 %collective-permute-start.6 = (bf16[64,2560]{1,0:T(8,128)(2,1)}, bf16[64,2560]{1,0:T(8,128)(2,1)S(1)}, u32[]{:S(2)}, u32[]{:S(2)}) collective-permute-start(bf16[64,2560]{1,0:T(8,128)(2,1)} %get-tuple-element.21), channel_id=1, source_target_pairs={{0,8},{1,9},{2,10},{3,11},{4,12},{5,13},{6,14},{7,15},{8,16},{9,17... | collective-permute-start | bytes 983048 | tf_op jit(solution)/shard_map/ppermute | solution.py:72
  33.4 0.7 collective-permute-start.7
  34.0 1.3 copy-done.8
  35.3 0.2 twice.1.refs_5_.refs_8_.refs_9_
  35.6 2.0 %activate.2.refs_6_.refs_9_.refs_15_.refs_14_ = f32[512,432]{1,0:T(8,128)S(1)} custom-call(s32[3]{0:T(128)S(1)} %pad_add_fusion.where, bf16[432,512]{1,0:T(8,128)(2,1)S(1)} %bitcast.48, bf16[432,512]{1,0:T(8,128)(2,1)S(1)} %bitcast.50, bf16[64,5120]{1,0:T(8,128)(2,1)} %pick.7.refs_3_.refs_2_.refs_1_), custom_call_target="tpu_custom_call" | custom-call | tf_op jit(solution)/shard_map/activate/pallas_call | solution.py:230
  37.8 2.6 %activate.3.refs_7_.refs_10_.refs_16_.refs_15_ = f32[512,432]{1,0:T(8,128)S(1)} custom-call(s32[3]{0:T(128)S(1)} %pad_add_fusion.where, bf16[432,640]{1,0:T(8,128)(2,1)} %collective-permute-done.12.refs_0_.refs_12_.refs_18_.refs_17_, bf16[64,5120]{1,0:T(8,128)(2,1)} %pick.7.refs_3_.refs_2_.refs_1_), custom_call_target="tpu_custom_call" | custom-call | tf_op jit(solution)/shard_map/activate/pallas_call | solution.py:230
  40.5 6.7 %collective-permute-done.8.refs_1_.refs_4_ = bf16[128,2560]{1,0:T(8,128)(2,1)S(1)} collective-permute-done((bf16[128,2560]{1,0:T(8,128)(2,1)}, bf16[128,2560]{1,0:T(8,128)(2,1)S(1)}, u32[]{:S(2)}, u32[]{:S(2)}) %collective-permute-start.8) | collective-permute-done | bytes 655392 | tf_op jit(solution)/shard_map/ppermute | solution.py:72
  47.5 1.5 collective-permute-start.15
  49.0 0.4 collective-permute-start.14
  49.6 12.1 %plane_pass.5.refs_3_.refs_18_ = f32[64,128]{1,0:T(8,128)S(1)} custom-call(s32[3]{0:T(128)S(1)} %pad_add_fusion.where, bf16[64,5120]{1,0:T(8,128)(2,1)S(1)} %assemble.1.refs_0_.refs_2_, bf16[64,5120]{1,0:T(8,128)(2,1)S(1)} %copy-done.3, bf16[64,5120]{1,0:T(8,128)(2,1)} %collective-permute-done.10.refs_4_.refs_2_, bf16[64,5120]{1,0:T(8,128)(2,1)S(1)} %copy-done.1, ...), custom_call_target="tpu_custom_call" | custom-call | tf_op jit(solution)/shard_map/plane_pass/pallas_call | solution.py:370
  61.8 0.3 collective-permute-done.15.refs_1_.refs_4_
  62.1 2.8 %collective-permute-done.16.refs_2_ = bf16[128,2560]{1,0:T(8,128)(2,1)S(1)} collective-permute-done((bf16[128,2560]{1,0:T(8,128)(2,1)S(1)}, bf16[128,2560]{1,0:T(8,128)(2,1)S(1)}, u32[]{:S(2)}, u32[]{:S(2)}) %collective-permute-start.16) | collective-permute-done | bytes 655392 | tf_op jit(solution)/shard_map/ppermute | solution.py:72
  65.1 2.1 %collective-permute-start.13 = (bf16[64,2560]{1,0:T(8,128)(2,1)S(1)}, bf16[64,2560]{1,0:T(8,128)(2,1)S(1)}, u32[]{:S(2)}, u32[]{:S(2)}) collective-permute-start(bf16[64,2560]{1,0:T(8,128)(2,1)S(1)} %pick.10.refs_13_), channel_id=1, source_target_pairs={{0,8},{1,9},{2,10},{3,11},{4,28},{5,29},{6,30},{7,31},{8,16},{9,17... | collective-permute-start | bytes 983048 | tf_op jit(solution)/shard_map/ppermute | solution.py:392
  67.2 2.3 %collective-permute-start.21 = (bf16[64,2560]{1,0:T(8,128)(2,1)S(1)}, bf16[64,2560]{1,0:T(8,128)(2,1)S(1)}, u32[]{:S(2)}, u32[]{:S(2)}) collective-permute-start(bf16[64,2560]{1,0:T(8,128)(2,1)S(1)} %collective-permute-done.20.refs_0_), channel_id=1, source_target_pairs={{0,1},{1,2},{2,3},{3,0},{4,5},{5,6},{6,7},{7,4},{8,9},{9,10},{10,1... | collective-permute-start | bytes 983048 | tf_op jit(solution)/shard_map/ppermute | solution.py:72
  69.6 0.2 collective-permute-start.22
  69.8 3.8 %collective-permute-done.14.refs_3_ = bf16[128,2560]{1,0:T(8,128)(2,1)S(1)} collective-permute-done((bf16[128,2560]{1,0:T(8,128)(2,1)S(1)}, bf16[128,2560]{1,0:T(8,128)(2,1)S(1)}, u32[]{:S(2)}, u32[]{:S(2)}) %collective-permute-start.14) | collective-permute-done | bytes 655392 | tf_op jit(solution)/shard_map/ppermute | solution.py:392
  73.7 7.1 %plane_pass.6 = (f32[256,432]{1,0:T(8,128)S(1)}, f32[256,432]{1,0:T(8,128)S(1)}, f32[256,432]{1,0:T(8,128)S(1)}, f32[256,432]{1,0:T(8,128)S(1)}, f32[512,128]{1,0:T(8,128)S(1)}) custom-call(s32[3]{0:T(128)S(1)} %pad_add_fusion.where, bf16[64,2560]{1,0:T(8,128)(2,1)S(1)} %copy-done.10, bf16[64,2560]{1,0:T(8,128)(2,1)S(1)} %copy-done.12, ...), custom_call_target="tpu_custom_call" | custom-call | tf_op jit(solution)/shard_map/plane_pass/pallas_call | solution.py:370
  80.9 2.7 %collective-permute-start.18 = (bf16[64,2560]{1,0:T(8,128)(2,1)S(1)}, bf16[64,2560]{1,0:T(8,128)(2,1)S(1)}, u32[]{:S(2)}, u32[]{:S(2)}) collective-permute-start(bf16[64,2560]{1,0:T(8,128)(2,1)S(1)} %hand.3.refs_3_.refs_0_), channel_id=1, source_target_pairs={{0,1},{1,2},{2,3},{3,0},{4,5},{5,6},{6,7},{7,4},{8,9},{9,10},{10,1... | collective-permute-start | bytes 983048 | tf_op jit(solution)/shard_map/ppermute | solution.py:72
  83.6 4.3 %collective-permute-done.22.refs_2_.refs_1_ = bf16[64,2560]{1,0:T(8,128)(2,1)S(1)} collective-permute-done((bf16[64,2560]{1,0:T(8,128)(2,1)S(1)}, bf16[64,2560]{1,0:T(8,128)(2,1)S(1)}, u32[]{:S(2)}, u32[]{:S(2)}) %collective-permute-start.22) | collective-permute-done | bytes 327712 | tf_op jit(solution)/shard_map/ppermute | solution.py:72
  88.1 8.4 %plane_pass.7.refs_3_.refs_19_ = f32[128,128]{1,0:T(8,128)S(1)} custom-call(s32[3]{0:T(128)S(1)} %pad_add_fusion.where, bf16[64,2560]{1,0:T(8,128)(2,1)S(1)} %collective-permute-done.7.refs_0_.refs_2_, bf16[64,2560]{1,0:T(8,128)(2,1)S(1)} %collective-permute-done.6.refs_1_, bf16[128,2560]{1,0:T(8,128)(2,1)S(1)} %collective-permute-done.16.refs_2_, ...), custom_call_target="tpu_custom_call" | custom-call | tf_op jit(solution)/shard_map/plane_pass/pallas_call | solution.py:370
  96.6 0.3 collective-permute-start.23
  97.0 1.3 collective-permute-done.24.refs_2_
  98.2 6.5 %plane_pass.8 = (f32[128,432]{1,0:T(8,128)S(1)}, f32[128,432]{1,0:T(8,128)S(1)}, f32[128,432]{1,0:T(8,128)S(1)}, f32[128,432]{1,0:T(8,128)S(1)}, f32[256,128]{1,0:T(8,128)S(1)}) custom-call(s32[3]{0:T(128)S(1)} %pad_add_fusion.where, bf16[64,2560]{1,0:T(8,128)(2,1)S(1)} %collective-permute-done.20.refs_0_, ...), custom_call_target="tpu_custom_call" | custom-call | tf_op jit(solution)/shard_map/plane_pass/pallas_call | solution.py:370
  104.8 7.2 %plane_pass.9 = (f32[4,16,128]{2,1,0:T(8,128)S(1)}, f32[4,16,128]{2,1,0:T(8,128)S(1)}, f32[4,16,128]{2,1,0:T(8,128)S(1)}, f32[4,16,128]{2,1,0:T(8,128)S(1)}) custom-call(s32[3]{0:T(128)S(1)} %pad_add_fusion.where, bf16[64,2560]{1,0:T(8,128)(2,1)S(1)} %hand.3.refs_3_.refs_0_, bf16[64,2560]{1,0:T(8,128)(2,1)S(1)} %collective-permute-done.17.refs_2_.refs_1_, ...), custom_call_target="tpu_custom_call" | custom-call | tf_op jit(solution)/shard_map/plane_pass/pallas_call | solution.py:370
  112.0 4.5 %collective-permute-start.25 = (f32[4,16,128]{2,1,0:T(8,128)S(1)}, f32[4,16,128]{2,1,0:T(8,128)S(1)}, u32[]{:S(2)}, u32[]{:S(2)}) collective-permute-start(f32[4,16,128]{2,1,0:T(8,128)S(1)} %get-tuple-element.34), channel_id=1, source_target_pairs={{0,16},{1,17},{2,18},{3,19},{4,20},{5,21},{6,22},{7,23},{8,24},{9,... | collective-permute-start | bytes 98312 | tf_op jit(solution)/shard_map/ppermute | solution.py:72
  116.5 2.4 %collective-permute-start.27 = (f32[4,16,128]{2,1,0:T(8,128)S(1)}, f32[4,16,128]{2,1,0:T(8,128)S(1)}, u32[]{:S(2)}, u32[]{:S(2)}) collective-permute-start(f32[4,16,128]{2,1,0:T(8,128)S(1)} %get-tuple-element.36), channel_id=1, source_target_pairs={{0,24},{1,25},{2,26},{3,27},{4,28},{5,29},{6,30},{7,31},{8,0},{9,1... | collective-permute-start | bytes 98312 | tf_op jit(solution)/shard_map/ppermute | solution.py:72
  118.9 1.6 %collective-permute-done.26 = f32[4,16,128]{2,1,0:T(8,128)S(1)} collective-permute-done((f32[4,16,128]{2,1,0:T(8,128)S(1)}, f32[4,16,128]{2,1,0:T(8,128)S(1)}, u32[]{:S(2)}, u32[]{:S(2)}) %collective-permute-start.26) | collective-permute-done | bytes 32800 | tf_op jit(solution)/shard_map/ppermute | solution.py:72
  120.5 1.2 collective-permute-done.27
  121.7 2.4 %collective-permute-start.28 = (f32[4,16,128]{2,1,0:T(8,128)S(1)}, f32[4,16,128]{2,1,0:T(8,128)S(1)}, u32[]{:S(2)}, u32[]{:S(2)}) collective-permute-start(f32[4,16,128]{2,1,0:T(8,128)S(1)} %add_add_fusion.1), channel_id=1, source_target_pairs={{0,2},{1,3},{2,0},{3,1},{4,6},{5,7},{6,4},{7,5},{8,10},{9,11},{10,... | collective-permute-start | bytes 98312 | tf_op jit(solution)/shard_map/ppermute | solution.py:72
  124.1 1.5 collective-permute-start.30
  125.6 0.5 collective-permute-done.28
  126.1 0.8 collective-permute-done.29
  126.9 1.2 collective-permute-done.30
  128.1 7.7 %collective-permute-start.31 = (f32[4,16,128]{2,1,0:T(8,128)S(1)}, f32[4,16,128]{2,1,0:T(8,128)S(1)}, u32[]{:S(2)}, u32[]{:S(2)}) collective-permute-start(f32[4,16,128]{2,1,0:T(8,128)S(1)} %add_add_fusion), channel_id=1, source_target_pairs={{0,4},{1,5},{2,6},{3,7},{4,0},{5,1},{6,2},{7,3},{8,12},{9,13},{10,... | collective-permute-start | bytes 98312 | tf_op jit(solution)/shard_map/ppermute | solution.py:72
  137.0 1.0 collective-permute-start.32
  137.9 1.9 %collective-permute-start.33 = (f32[1,4]{1,0:T(1,128)S(1)}, f32[1,4]{1,0:T(1,128)S(1)}, u32[]{:S(2)}, u32[]{:S(2)}) collective-permute-start(f32[1,4]{1,0:T(1,128)S(1)} %dynamic-slice_bitcast_fusion), channel_id=1, source_target_pairs={{0,32},{32,64},{64,96},{96,0},{128,160},{160,192},{192,224},{224,1... | collective-permute-start | bytes 56 | tf_op jit(solution)/shard_map/ppermute | solution.py:501
  139.8 1.0 collective-permute-done.32
  140.9 2.6 %collective-permute-done.34 = f32[1,4]{1,0:T(1,128)S(1)} collective-permute-done((f32[1,4]{1,0:T(1,128)S(1)}, f32[1,4]{1,0:T(1,128)S(1)}, u32[]{:S(2)}, u32[]{:S(2)}) %collective-permute-start.34) | collective-permute-done | bytes 48 | tf_op jit(solution)/shard_map/ppermute | solution.py:501
  143.5 3.3 %collective-permute-start.35 = (f32[1,4]{1,0:T(1,128)S(1)}, f32[1,4]{1,0:T(1,128)S(1)}, u32[]{:S(2)}, u32[]{:S(2)}) collective-permute-start(f32[1,4]{1,0:T(1,128)S(1)} %add_add_fusion.2), channel_id=1, source_target_pairs={{0,16},{1,17},{2,18},{3,19},{4,132},{5,133},{6,134},{7,135},{32,48... | collective-permute-start | bytes 56 | tf_op jit(solution)/shard_map/ppermute | solution.py:503
  146.8 0.9 collective-permute-start.36
  147.6 3.6 %collective-permute-start.37 = (f32[1,4]{1,0:T(1,128)S(1)}, f32[1,4]{1,0:T(1,128)S(1)}, u32[]{:S(2)}, u32[]{:S(2)}) collective-permute-start(f32[1,4]{1,0:T(1,128)S(1)} %add_add_fusion.2), channel_id=1, source_target_pairs={{0,24},{1,25},{2,26},{3,27},{4,140},{5,141},{6,142},{7,143},{32,56... | collective-permute-start | bytes 56 | tf_op jit(solution)/shard_map/ppermute | solution.py:503
  151.3 1.9 %collective-permute-start.38 = (f32[1,4]{1,0:T(1,128)S(1)}, f32[1,4]{1,0:T(1,128)S(1)}, u32[]{:S(2)}, u32[]{:S(2)}) collective-permute-start(f32[1,4]{1,0:T(1,128)S(1)} %add_add_fusion.2), channel_id=1, source_target_pairs={{4,156},{5,157},{6,158},{7,159},{36,188},{37,189},{38,190},{39,191... | collective-permute-start | bytes 56 | tf_op jit(solution)/shard_map/ppermute | solution.py:503
  153.2 2.3 %collective-permute-done.38 = f32[1,4]{1,0:T(1,128)S(1)} collective-permute-done((f32[1,4]{1,0:T(1,128)S(1)}, f32[1,4]{1,0:T(1,128)S(1)}, u32[]{:S(2)}, u32[]{:S(2)}) %collective-permute-start.38) | collective-permute-done | bytes 48 | tf_op jit(solution)/shard_map/ppermute | solution.py:503
  155.5 1.4 collective-permute-start.39
  156.9 0.8 collective-permute-done.39
  157.7 0.5 add.80
  (89 shorter events, 2.4 us)
Async XLA Ops:
  1.2 2.0 %collective-permute-start = (bf16[32,5120]{1,0:T(8,128)(2,1)S(1)}, bf16[32,5120]{1,0:T(8,128)(2,1)S(1)}, u32[]{:S(2)}, u32[]{:S(2)}) collective-permute-start(bf16[32,5120]{1,0:T(8,128)(2,1)S(1)} %pad_maximum_fusion.1), channel_id=1, source_target_pairs={{0,4},{1,5},{2,6},{3,7},{4,0},{5,1},{6,2},{7,3},{8,12},{9,13},{10,... | collective-permute-start | bytes 983048 | tf_op jit(solution)/shard_map/ppermute | solution.py:72
  2.0 7.9 %collective-permute-start.1 = (bf16[432,5120]{1,0:T(8,128)(2,1)}, bf16[432,5120]{1,0:T(8,128)(2,1)}, u32[]{:S(2)}, u32[]{:S(2)}) collective-permute-start(bf16[432,5120]{1,0:T(8,128)(2,1)} %bitcast.31), channel_id=1, source_target_pairs={{0,4},{1,5},{2,6},{3,7},{4,0},{5,1},{6,2},{7,3},{8,12},{9,13},{10,... | collective-permute-start | bytes 13271048 | tf_op jit(solution)/shard_map/ppermute | solution.py:72
  2.1 20.3 %collective-permute-start.11 = (bf16[432,5120]{1,0:T(8,128)(2,1)}, bf16[432,5120]{1,0:T(8,128)(2,1)}, u32[]{:S(2)}, u32[]{:S(2)}) collective-permute-start(bf16[432,5120]{1,0:T(8,128)(2,1)} %bitcast.39), channel_id=1, source_target_pairs={{0,4},{1,5},{2,6},{3,7},{4,0},{5,1},{6,2},{7,3},{8,12},{9,13},{10,... | collective-permute-start | bytes 13271048 | tf_op jit(solution)/shard_map/ppermute | solution.py:72
  3.3 19.1 %copy-start.4 = (bf16[1,512,432]{1,2,0:T(8,128)(2,1)S(1)}, bf16[1,512,432]{1,2,0:T(8,128)(2,1)}, u32[]{:S(2)}) copy-start(bf16[1,512,432]{1,2,0:T(8,128)(2,1)} %param.15) | copy-start | bytes 1327108
  3.3 19.1 %copy-start.6 = (bf16[1,512,432]{1,2,0:T(8,128)(2,1)S(1)}, bf16[1,512,432]{1,2,0:T(8,128)(2,1)}, u32[]{:S(2)}) copy-start(bf16[1,512,432]{1,2,0:T(8,128)(2,1)} %param.16) | copy-start | bytes 1327108
  3.3 19.1 %copy-start.13 = (s32[432,64]{0,1:T(8,128)S(1)}, s32[432,64]{0,1:T(8,128)}, u32[]{:S(2)}) copy-start(s32[432,64]{0,1:T(8,128)} %param.19) | copy-start | bytes 331780
  3.3 16.0 %collective-permute-start.4 = (bf16[64,5120]{1,0:T(8,128)(2,1)S(1)}, bf16[64,5120]{1,0:T(8,128)(2,1)S(1)}, u32[]{:S(2)}, u32[]{:S(2)}) collective-permute-start(bf16[64,5120]{1,0:T(8,128)(2,1)S(1)} %assemble.1.refs_0_.refs_2_), channel_id=1, source_target_pairs={{0,1},{1,2},{2,3},{3,0},{4,5},{5,6},{6,7},{7,4},{8,9},{9,10},{10,1... | collective-permute-start | bytes 1966088 | tf_op jit(solution)/shard_map/ppermute | solution.py:72
  3.6 16.8 %collective-permute-start.5 = (bf16[64,5120]{1,0:T(8,128)(2,1)S(1)}, bf16[64,5120]{1,0:T(8,128)(2,1)S(1)}, u32[]{:S(2)}, u32[]{:S(2)}) collective-permute-start(bf16[64,5120]{1,0:T(8,128)(2,1)S(1)} %assemble.1.refs_0_.refs_2_), channel_id=1, source_target_pairs={{0,3},{1,0},{2,1},{3,2},{4,7},{5,4},{6,5},{7,6},{8,11},{9,8},{10,9... | collective-permute-start | bytes 1966088 | tf_op jit(solution)/shard_map/ppermute | solution.py:72
  9.9 19.1 %collective-permute-start.2 = (bf16[64,2560]{1,0:T(8,128)(2,1)S(1)}, bf16[64,2560]{1,0:T(8,128)(2,1)S(1)}, u32[]{:S(2)}, u32[]{:S(2)}) collective-permute-start(bf16[64,2560]{1,0:T(8,128)(2,1)S(1)} %hand.2), channel_id=1, source_target_pairs={{0,24},{1,25},{2,26},{3,27},{4,28},{5,29},{6,30},{7,31},{8,0},{9,1... | collective-permute-start | bytes 983048 | tf_op jit(solution)/shard_map/ppermute | solution.py:72
  10.0 19.0 %collective-permute-start.3 = (bf16[64,2560]{1,0:T(8,128)(2,1)S(1)}, bf16[64,2560]{1,0:T(8,128)(2,1)S(1)}, u32[]{:S(2)}, u32[]{:S(2)}) collective-permute-start(bf16[64,2560]{1,0:T(8,128)(2,1)S(1)} %hand.2), channel_id=1, source_target_pairs={{0,8},{1,9},{2,10},{3,11},{4,12},{5,13},{6,14},{7,15},{8,16},{9,17... | collective-permute-start | bytes 983048 | tf_op jit(solution)/shard_map/ppermute | solution.py:72
  20.4 9.6 %copy-start.2 = (bf16[64,5120]{1,0:T(8,128)(2,1)}, bf16[64,5120]{1,0:T(8,128)(2,1)S(1)}, u32[]{:S(2)}) copy-start(bf16[64,5120]{1,0:T(8,128)(2,1)S(1)} %collective-permute-done.5.refs_2_.refs_1_) | copy-start | bytes 1966084
  21.5 0.8 copy-start
  22.3 18.2 %collective-permute-start.10 = (bf16[64,5120]{1,0:T(8,128)(2,1)}, bf16[64,5120]{1,0:T(8,128)(2,1)}, u32[]{:S(2)}, u32[]{:S(2)}) collective-permute-start(bf16[64,5120]{1,0:T(8,128)(2,1)} %pick.7.refs_3_.refs_2_.refs_1_), channel_id=1, source_target_pairs={{0,1},{1,2},{2,3},{3,0},{4,7},{5,4},{6,5},{7,6},{8,9},{9,10},{10,1... | collective-permute-start | bytes 1966088 | tf_op jit(solution)/shard_map/ppermute | solution.py:392
  23.4 9.9 %collective-permute-start.12 = (bf16[432,640]{1,0:T(8,128)(2,1)}, bf16[432,640]{1,0:T(8,128)(2,1)}, u32[]{:S(2)}, u32[]{:S(2)}) collective-permute-start(bf16[432,640]{1,0:T(8,128)(2,1)} %pack.1.refs_11_.refs_17_.refs_16_), channel_id=1, source_target_pairs={{0,4},{1,5},{2,6},{3,7},{4,0},{5,1},{6,2},{7,3},{8,12},{9,13},{10,... | collective-permute-start | bytes 1658888 | tf_op jit(solution)/shard_map/ppermute | solution.py:72
  29.0 1.1 copy-start.9
  29.0 1.1 copy-start.11
  29.0 6.6 %copy-start.5 = (bf16[1,512,432]{1,2,0:T(8,128)(2,1)S(1)}, bf16[1,512,432]{1,2,0:T(8,128)(2,1)}, u32[]{:S(2)}) copy-start(bf16[1,512,432]{1,2,0:T(8,128)(2,1)} %param.15) | copy-start | bytes 1327108
  29.0 6.6 %copy-start.7 = (bf16[1,512,432]{1,2,0:T(8,128)(2,1)S(1)}, bf16[1,512,432]{1,2,0:T(8,128)(2,1)}, u32[]{:S(2)}) copy-start(bf16[1,512,432]{1,2,0:T(8,128)(2,1)} %param.16) | copy-start | bytes 1327108
  30.2 17.0 %collective-permute-start.8 = (bf16[128,2560]{1,0:T(8,128)(2,1)}, bf16[128,2560]{1,0:T(8,128)(2,1)S(1)}, u32[]{:S(2)}, u32[]{:S(2)}) collective-permute-start(bf16[128,2560]{1,0:T(8,128)(2,1)} %get-tuple-element.22.refs_3_), channel_id=1, source_target_pairs={{0,1},{1,2},{2,3},{3,0},{4,5},{5,6},{6,7},{7,4},{8,9},{9,10},{10,1... | collective-permute-start | bytes 1966088 | tf_op jit(solution)/shard_map/ppermute | solution.py:72
  30.4 16.8 %collective-permute-start.9 = (bf16[128,2560]{1,0:T(8,128)(2,1)}, bf16[128,2560]{1,0:T(8,128)(2,1)S(1)}, u32[]{:S(2)}, u32[]{:S(2)}) collective-permute-start(bf16[128,2560]{1,0:T(8,128)(2,1)} %get-tuple-element.22.refs_3_), channel_id=1, source_target_pairs={{0,3},{1,0},{2,1},{3,2},{4,7},{5,4},{6,5},{7,6},{8,11},{9,8},{10,9... | collective-permute-start | bytes 1966088 | tf_op jit(solution)/shard_map/ppermute | solution.py:72
  31.7 15.8 %collective-permute-start.6 = (bf16[64,2560]{1,0:T(8,128)(2,1)}, bf16[64,2560]{1,0:T(8,128)(2,1)S(1)}, u32[]{:S(2)}, u32[]{:S(2)}) collective-permute-start(bf16[64,2560]{1,0:T(8,128)(2,1)} %get-tuple-element.21), channel_id=1, source_target_pairs={{0,8},{1,9},{2,10},{3,11},{4,12},{5,13},{6,14},{7,15},{8,16},{9,17... | collective-permute-start | bytes 983048 | tf_op jit(solution)/shard_map/ppermute | solution.py:72
  33.4 14.1 %collective-permute-start.7 = (bf16[64,2560]{1,0:T(8,128)(2,1)}, bf16[64,2560]{1,0:T(8,128)(2,1)S(1)}, u32[]{:S(2)}, u32[]{:S(2)}) collective-permute-start(bf16[64,2560]{1,0:T(8,128)(2,1)} %get-tuple-element.21), channel_id=1, source_target_pairs={{0,24},{1,25},{2,26},{3,27},{4,28},{5,29},{6,30},{7,31},{8,0},{9,1... | collective-permute-start | bytes 983048 | tf_op jit(solution)/shard_map/ppermute | solution.py:72
  34.0 1.3 copy-start.8
  35.3 2.3 %copy-start.10 = (bf16[64,2560]{1,0:T(8,128)(2,1)S(1)}, bf16[64,2560]{1,0:T(8,128)(2,1)}, u32[]{:S(2)}) copy-start(bf16[64,2560]{1,0:T(8,128)(2,1)} %copy-done.9) | copy-start | bytes 983044
  35.3 2.3 %copy-start.12 = (bf16[64,2560]{1,0:T(8,128)(2,1)S(1)}, bf16[64,2560]{1,0:T(8,128)(2,1)}, u32[]{:S(2)}) copy-start(bf16[64,2560]{1,0:T(8,128)(2,1)} %copy-done.11) | copy-start | bytes 983044
  37.7 11.9 %slice-start.2 = ((s8[4423680]{0:T(1024)(128)(4,1)}), s8[4194304]{0:T(1024)(128)(4,1)S(1)}, s32[]{:S(2)}) async-start(s8[4423680]{0:T(1024)(128)(4,1)} %bitcast.40), calls=%async_computation.2 | async-start | bytes 8388608
  37.8 11.8 %slice-start = ((s8[4423680]{0:T(1024)(128)(4,1)}), s8[4194304]{0:T(1024)(128)(4,1)S(1)}, s32[]{:S(2)}) async-start(s8[4423680]{0:T(1024)(128)(4,1)} %bitcast.32), calls=%async_computation | async-start | bytes 8388608
  40.5 9.1 %slice-start.1 = ((s8[4423680]{0:T(1024)(128)(4,1)}), s8[229376]{0:T(1024)(128)(4,1)S(1)}, s32[]{:S(2)}) async-start(s8[4423680]{0:T(1024)(128)(4,1)} %bitcast.32), calls=%async_computation.1 | async-start | bytes 458752
  40.5 9.1 %slice-start.3 = ((s8[4423680]{0:T(1024)(128)(4,1)}), s8[229376]{0:T(1024)(128)(4,1)S(1)}, s32[]{:S(2)}) async-start(s8[4423680]{0:T(1024)(128)(4,1)} %bitcast.40), calls=%async_computation.3 | async-start | bytes 458752
  40.5 9.1 %copy-start.1 = (bf16[64,5120]{1,0:T(8,128)(2,1)S(1)}, bf16[64,5120]{1,0:T(8,128)(2,1)}, u32[]{:S(2)}) copy-start(bf16[64,5120]{1,0:T(8,128)(2,1)} %copy-done) | copy-start | bytes 1966084
  40.5 9.1 %copy-start.3 = (bf16[64,5120]{1,0:T(8,128)(2,1)S(1)}, bf16[64,5120]{1,0:T(8,128)(2,1)}, u32[]{:S(2)}) copy-start(bf16[64,5120]{1,0:T(8,128)(2,1)} %copy-done.2) | copy-start | bytes 1966084
  47.5 14.6 %collective-permute-start.15 = (bf16[128,2560]{1,0:T(8,128)(2,1)S(1)}, bf16[128,2560]{1,0:T(8,128)(2,1)S(1)}, u32[]{:S(2)}, u32[]{:S(2)}) collective-permute-start(bf16[128,2560]{1,0:T(8,128)(2,1)S(1)} %regroup.3.refs_3_), channel_id=1, source_target_pairs={{0,1},{1,2},{2,3},{3,0},{4,5},{5,6},{6,7},{7,4},{8,9},{9,10},{10,1... | collective-permute-start | bytes 1966088 | tf_op jit(solution)/shard_map/ppermute | solution.py:72
  49.0 15.8 %collective-permute-start.16 = (bf16[128,2560]{1,0:T(8,128)(2,1)S(1)}, bf16[128,2560]{1,0:T(8,128)(2,1)S(1)}, u32[]{:S(2)}, u32[]{:S(2)}) collective-permute-start(bf16[128,2560]{1,0:T(8,128)(2,1)S(1)} %regroup.3.refs_3_), channel_id=1, source_target_pairs={{0,3},{1,0},{2,1},{3,2},{4,7},{5,4},{6,5},{7,6},{8,11},{9,8},{10,9... | collective-permute-start | bytes 1966088 | tf_op jit(solution)/shard_map/ppermute | solution.py:72
  49.0 24.6 %collective-permute-start.14 = (bf16[128,2560]{1,0:T(8,128)(2,1)S(1)}, bf16[128,2560]{1,0:T(8,128)(2,1)S(1)}, u32[]{:S(2)}, u32[]{:S(2)}) collective-permute-start(bf16[128,2560]{1,0:T(8,128)(2,1)S(1)} %pick.9.refs_2_), channel_id=1, source_target_pairs={{0,1},{1,2},{2,3},{3,0},{4,7},{5,4},{6,5},{7,6},{8,9},{9,10},{10,1... | collective-permute-start | bytes 1966088 | tf_op jit(solution)/shard_map/ppermute | solution.py:392
  49.5 17.8 %collective-permute-start.20 = (bf16[64,2560]{1,0:T(8,128)(2,1)S(1)}, bf16[64,2560]{1,0:T(8,128)(2,1)S(1)}, u32[]{:S(2)}, u32[]{:S(2)}) collective-permute-start(bf16[64,2560]{1,0:T(8,128)(2,1)S(1)} %pick.8.refs_3_), channel_id=1, source_target_pairs={{0,8},{1,9},{2,10},{3,11},{4,28},{5,29},{6,30},{7,31},{8,16},{9,17... | collective-permute-start | bytes 983048 | tf_op jit(solution)/shard_map/ppermute | solution.py:392
  65.0 23.1 %collective-permute-start.19 = (bf16[128,2560]{1,0:T(8,128)(2,1)S(1)}, bf16[128,2560]{1,0:T(8,128)(2,1)S(1)}, u32[]{:S(2)}, u32[]{:S(2)}) collective-permute-start(bf16[128,2560]{1,0:T(8,128)(2,1)S(1)} %pick.11.refs_10_), channel_id=1, source_target_pairs={{0,1},{1,2},{2,3},{3,0},{4,7},{5,4},{6,5},{7,6},{8,9},{9,10},{10,1... | collective-permute-start | bytes 1966088 | tf_op jit(solution)/shard_map/ppermute | solution.py:392
  65.1 15.7 %collective-permute-start.13 = (bf16[64,2560]{1,0:T(8,128)(2,1)S(1)}, bf16[64,2560]{1,0:T(8,128)(2,1)S(1)}, u32[]{:S(2)}, u32[]{:S(2)}) collective-permute-start(bf16[64,2560]{1,0:T(8,128)(2,1)S(1)} %pick.10.refs_13_), channel_id=1, source_target_pairs={{0,8},{1,9},{2,10},{3,11},{4,28},{5,29},{6,30},{7,31},{8,16},{9,17... | collective-permute-start | bytes 983048 | tf_op jit(solution)/shard_map/ppermute | solution.py:392
  67.2 16.4 %collective-permute-start.21 = (bf16[64,2560]{1,0:T(8,128)(2,1)S(1)}, bf16[64,2560]{1,0:T(8,128)(2,1)S(1)}, u32[]{:S(2)}, u32[]{:S(2)}) collective-permute-start(bf16[64,2560]{1,0:T(8,128)(2,1)S(1)} %collective-permute-done.20.refs_0_), channel_id=1, source_target_pairs={{0,1},{1,2},{2,3},{3,0},{4,5},{5,6},{6,7},{7,4},{8,9},{9,10},{10,1... | collective-permute-start | bytes 983048 | tf_op jit(solution)/shard_map/ppermute | solution.py:72
  69.6 18.4 %collective-permute-start.22 = (bf16[64,2560]{1,0:T(8,128)(2,1)S(1)}, bf16[64,2560]{1,0:T(8,128)(2,1)S(1)}, u32[]{:S(2)}, u32[]{:S(2)}) collective-permute-start(bf16[64,2560]{1,0:T(8,128)(2,1)S(1)} %collective-permute-done.20.refs_0_), channel_id=1, source_target_pairs={{0,3},{1,0},{2,1},{3,2},{4,7},{5,4},{6,5},{7,6},{8,11},{9,8},{10,9... | collective-permute-start | bytes 983048 | tf_op jit(solution)/shard_map/ppermute | solution.py:72
  80.8 15.7 %collective-permute-start.17 = (bf16[64,2560]{1,0:T(8,128)(2,1)S(1)}, bf16[64,2560]{1,0:T(8,128)(2,1)S(1)}, u32[]{:S(2)}, u32[]{:S(2)}) collective-permute-start(bf16[64,2560]{1,0:T(8,128)(2,1)S(1)} %hand.3.refs_3_.refs_0_), channel_id=1, source_target_pairs={{0,3},{1,0},{2,1},{3,2},{4,7},{5,4},{6,5},{7,6},{8,11},{9,8},{10,9... | collective-permute-start | bytes 983048 | tf_op jit(solution)/shard_map/ppermute | solution.py:72
  80.9 15.6 %collective-permute-start.18 = (bf16[64,2560]{1,0:T(8,128)(2,1)S(1)}, bf16[64,2560]{1,0:T(8,128)(2,1)S(1)}, u32[]{:S(2)}, u32[]{:S(2)}) collective-permute-start(bf16[64,2560]{1,0:T(8,128)(2,1)S(1)} %hand.3.refs_3_.refs_0_), channel_id=1, source_target_pairs={{0,1},{1,2},{2,3},{3,0},{4,5},{5,6},{6,7},{7,4},{8,9},{9,10},{10,1... | collective-permute-start | bytes 983048 | tf_op jit(solution)/shard_map/ppermute | solution.py:72
  88.0 10.2 %collective-permute-start.24 = (bf16[64,2560]{1,0:T(8,128)(2,1)S(1)}, bf16[64,2560]{1,0:T(8,128)(2,1)S(1)}, u32[]{:S(2)}, u32[]{:S(2)}) collective-permute-start(bf16[64,2560]{1,0:T(8,128)(2,1)S(1)} %pick.12.refs_19_), channel_id=1, source_target_pairs={{0,1},{1,2},{2,3},{3,0},{4,7},{5,4},{6,5},{7,6},{8,9},{9,10},{10,1... | collective-permute-start | bytes 983048 | tf_op jit(solution)/shard_map/ppermute | solution.py:392
  96.6 8.1 %collective-permute-start.23 = (bf16[64,2560]{1,0:T(8,128)(2,1)S(1)}, bf16[64,2560]{1,0:T(8,128)(2,1)S(1)}, u32[]{:S(2)}, u32[]{:S(2)}) collective-permute-start(bf16[64,2560]{1,0:T(8,128)(2,1)S(1)} %pick.13.refs_9_), channel_id=1, source_target_pairs={{0,1},{1,2},{2,3},{3,0},{4,7},{5,4},{6,5},{7,6},{8,9},{9,10},{10,1... | collective-permute-start | bytes 983048 | tf_op jit(solution)/shard_map/ppermute | solution.py:392
  112.0 6.9 %collective-permute-start.25 = (f32[4,16,128]{2,1,0:T(8,128)S(1)}, f32[4,16,128]{2,1,0:T(8,128)S(1)}, u32[]{:S(2)}, u32[]{:S(2)}) collective-permute-start(f32[4,16,128]{2,1,0:T(8,128)S(1)} %get-tuple-element.34), channel_id=1, source_target_pairs={{0,16},{1,17},{2,18},{3,19},{4,20},{5,21},{6,22},{7,23},{8,24},{9,... | collective-permute-start | bytes 98312 | tf_op jit(solution)/shard_map/ppermute | solution.py:72
  116.5 4.0 %collective-permute-start.26 = (f32[4,16,128]{2,1,0:T(8,128)S(1)}, f32[4,16,128]{2,1,0:T(8,128)S(1)}, u32[]{:S(2)}, u32[]{:S(2)}) collective-permute-start(f32[4,16,128]{2,1,0:T(8,128)S(1)} %get-tuple-element.35), channel_id=1, source_target_pairs={{0,8},{1,9},{2,10},{3,11},{4,12},{5,13},{6,14},{7,15},{8,16},{9,17... | collective-permute-start | bytes 98312 | tf_op jit(solution)/shard_map/ppermute | solution.py:72
  116.5 5.2 %collective-permute-start.27 = (f32[4,16,128]{2,1,0:T(8,128)S(1)}, f32[4,16,128]{2,1,0:T(8,128)S(1)}, u32[]{:S(2)}, u32[]{:S(2)}) collective-permute-start(f32[4,16,128]{2,1,0:T(8,128)S(1)} %get-tuple-element.36), channel_id=1, source_target_pairs={{0,24},{1,25},{2,26},{3,27},{4,28},{5,29},{6,30},{7,31},{8,0},{9,1... | collective-permute-start | bytes 98312 | tf_op jit(solution)/shard_map/ppermute | solution.py:72
  121.7 4.4 %collective-permute-start.28 = (f32[4,16,128]{2,1,0:T(8,128)S(1)}, f32[4,16,128]{2,1,0:T(8,128)S(1)}, u32[]{:S(2)}, u32[]{:S(2)}) collective-permute-start(f32[4,16,128]{2,1,0:T(8,128)S(1)} %add_add_fusion.1), channel_id=1, source_target_pairs={{0,2},{1,3},{2,0},{3,1},{4,6},{5,7},{6,4},{7,5},{8,10},{9,11},{10,... | collective-permute-start | bytes 98312 | tf_op jit(solution)/shard_map/ppermute | solution.py:72
  124.1 2.8 %collective-permute-start.29 = (f32[4,16,128]{2,1,0:T(8,128)S(1)}, f32[4,16,128]{2,1,0:T(8,128)S(1)}, u32[]{:S(2)}, u32[]{:S(2)}) collective-permute-start(f32[4,16,128]{2,1,0:T(8,128)S(1)} %add_add_fusion.1), channel_id=1, source_target_pairs={{0,1},{1,2},{2,3},{3,0},{4,5},{5,6},{6,7},{7,4},{8,9},{9,10},{10,1... | collective-permute-start | bytes 98312 | tf_op jit(solution)/shard_map/ppermute | solution.py:72
  124.1 4.0 %collective-permute-start.30 = (f32[4,16,128]{2,1,0:T(8,128)S(1)}, f32[4,16,128]{2,1,0:T(8,128)S(1)}, u32[]{:S(2)}, u32[]{:S(2)}) collective-permute-start(f32[4,16,128]{2,1,0:T(8,128)S(1)} %add_add_fusion.1), channel_id=1, source_target_pairs={{0,3},{1,0},{2,1},{3,2},{4,7},{5,4},{6,5},{7,6},{8,11},{9,8},{10,9... | collective-permute-start | bytes 98312 | tf_op jit(solution)/shard_map/ppermute | solution.py:72
  128.1 8.6 %collective-permute-start.31 = (f32[4,16,128]{2,1,0:T(8,128)S(1)}, f32[4,16,128]{2,1,0:T(8,128)S(1)}, u32[]{:S(2)}, u32[]{:S(2)}) collective-permute-start(f32[4,16,128]{2,1,0:T(8,128)S(1)} %add_add_fusion), channel_id=1, source_target_pairs={{0,4},{1,5},{2,6},{3,7},{4,0},{5,1},{6,2},{7,3},{8,12},{9,13},{10,... | collective-permute-start | bytes 98312 | tf_op jit(solution)/shard_map/ppermute | solution.py:72
  137.0 3.9 %collective-permute-start.32 = (f32[1,4]{1,0:T(1,128)S(1)}, f32[1,4]{1,0:T(1,128)S(1)}, u32[]{:S(2)}, u32[]{:S(2)}) collective-permute-start(f32[1,4]{1,0:T(1,128)S(1)} %dynamic-slice_bitcast_fusion), channel_id=1, source_target_pairs={{0,64},{32,96},{64,0},{96,32},{128,192},{160,224},{192,128},{224,1... | collective-permute-start | bytes 56 | tf_op jit(solution)/shard_map/ppermute | solution.py:501
  137.9 2.9 %collective-permute-start.33 = (f32[1,4]{1,0:T(1,128)S(1)}, f32[1,4]{1,0:T(1,128)S(1)}, u32[]{:S(2)}, u32[]{:S(2)}) collective-permute-start(f32[1,4]{1,0:T(1,128)S(1)} %dynamic-slice_bitcast_fusion), channel_id=1, source_target_pairs={{0,32},{32,64},{64,96},{96,0},{128,160},{160,192},{192,224},{224,1... | collective-permute-start | bytes 56 | tf_op jit(solution)/shard_map/ppermute | solution.py:501
  139.8 3.6 %collective-permute-start.34 = (f32[1,4]{1,0:T(1,128)S(1)}, f32[1,4]{1,0:T(1,128)S(1)}, u32[]{:S(2)}, u32[]{:S(2)}) collective-permute-start(f32[1,4]{1,0:T(1,128)S(1)} %dynamic-slice_bitcast_fusion), channel_id=1, source_target_pairs={{0,96},{32,0},{64,32},{96,64},{128,224},{160,128},{192,160},{224,1... | collective-permute-start | bytes 56 | tf_op jit(solution)/shard_map/ppermute | solution.py:501
  143.5 9.7 %collective-permute-start.35 = (f32[1,4]{1,0:T(1,128)S(1)}, f32[1,4]{1,0:T(1,128)S(1)}, u32[]{:S(2)}, u32[]{:S(2)}) collective-permute-start(f32[1,4]{1,0:T(1,128)S(1)} %add_add_fusion.2), channel_id=1, source_target_pairs={{0,16},{1,17},{2,18},{3,19},{4,132},{5,133},{6,134},{7,135},{32,48... | collective-permute-start | bytes 56 | tf_op jit(solution)/shard_map/ppermute | solution.py:503
  146.8 6.4 %collective-permute-start.36 = (f32[1,4]{1,0:T(1,128)S(1)}, f32[1,4]{1,0:T(1,128)S(1)}, u32[]{:S(2)}, u32[]{:S(2)}) collective-permute-start(f32[1,4]{1,0:T(1,128)S(1)} %add_add_fusion.2), channel_id=1, source_target_pairs={{0,8},{1,9},{2,10},{3,11},{4,148},{5,149},{6,150},{7,151},{32,40},... | collective-permute-start | bytes 56 | tf_op jit(solution)/shard_map/ppermute | solution.py:503
  147.6 5.6 %collective-permute-start.37 = (f32[1,4]{1,0:T(1,128)S(1)}, f32[1,4]{1,0:T(1,128)S(1)}, u32[]{:S(2)}, u32[]{:S(2)}) collective-permute-start(f32[1,4]{1,0:T(1,128)S(1)} %add_add_fusion.2), channel_id=1, source_target_pairs={{0,24},{1,25},{2,26},{3,27},{4,140},{5,141},{6,142},{7,143},{32,56... | collective-permute-start | bytes 56 | tf_op jit(solution)/shard_map/ppermute | solution.py:503
  151.3 4.3 %collective-permute-start.38 = (f32[1,4]{1,0:T(1,128)S(1)}, f32[1,4]{1,0:T(1,128)S(1)}, u32[]{:S(2)}, u32[]{:S(2)}) collective-permute-start(f32[1,4]{1,0:T(1,128)S(1)} %add_add_fusion.2), channel_id=1, source_target_pairs={{4,156},{5,157},{6,158},{7,159},{36,188},{37,189},{38,190},{39,191... | collective-permute-start | bytes 56 | tf_op jit(solution)/shard_map/ppermute | solution.py:503
  155.5 2.2 %collective-permute-start.39 = (f32[1,4]{1,0:T(1,128)S(1)}, f32[1,4]{1,0:T(1,128)S(1)}, u32[]{:S(2)}, u32[]{:S(2)}) collective-permute-start(f32[1,4]{1,0:T(1,128)S(1)} %broadcast_select_fusion), channel_id=1, source_target_pairs={{0,4},{1,5},{2,6},{3,7},{4,0},{5,1},{6,2},{7,3},{8,12},{9,13},{10,... | collective-permute-start | bytes 56 | tf_op jit(solution)/shard_map/ppermute | solution.py:72
where the time goes:
time: 159 us; the launch traced here: 158 us
  starting transfers between devices  55.1 us (35%)
  Pallas kernels  50.2 us (32%)
  waiting for transfers between devices  47.2 us (30%)
  local copies, waits for them, and re-layouts  2.42 us (2%)
  other arithmetic  2.15 us (1%)
    pallas_call x5, Pallas kernels, plane_pass(): pl.pallas_call(kernel, name='plane_pass', grid_spec=pltpu.PrefetchScalarG...  41.4 us
    ppermute x26, starting transfers between devices, move(): return lax.ppermute(a, GROUP, group_pairs(dz, dc, dx))  39.4 us
    ppermute x26, waiting for transfers between devices, move(): return lax.ppermute(a, GROUP, group_pairs(dz, dc, dx))  36.2 us
    ppermute x4, starting transfers between devices, body(): line = lambda d0, d1: lax.ppermute(block, EVERY, z_pairs(d0, d1))  9.66 us
    ppermute x7, waiting for transfers between devices, across(): return lax.ppermute(a, GROUP, opposed_pairs(dz, dx))  5.15 us
    pallas_call x2, Pallas kernels, activate(): pl.pallas_call(kernel, name='activate', grid=(1,), in_specs=[SM] + [pl.Bl...  4.66 us
    pallas_call x14, Pallas kernels, call(): pl.pallas_call(run, name=name, in_specs=list(specs) + [ANY] * (n_dep + n_...  4.17 us
    ppermute x3, waiting for transfers between devices, body(): ckpt = lambda v, d: lax.ppermute(v, ('ckpt',), y_pairs(d))  3.6 us
  transfers between devices with their start and end apart: 40, of which 21 were waited for; matrix products, arithmetic and copies ran while one was open for 0% of the time, Pallas kernels for 27%

commit v1 on v0

--- a/solution.py
+++ b/solution.py
@@ -12,7 +12,6 @@
 SEQ = 128
 ROWS = 512
 UNITS = 432
-STEP = 512
 HALF = D // 2
 PACKED = ROWS + 128
 GROUP = ("zhi", "core", "ex")
@@ -266,9 +265,10 @@
     f32 = jnp.float32
     rows = planes[1] * SEQ
     first, planes = planes
-    steps = D // STEP if half is None else HALF // STEP
+    last = before is not None
+    width = 1280 if last else 512
+    steps = D // width if half is None else HALF // width
     skip = steps if half == 1 else 0
-    last = before is not None
     ends = half != 0
     n_sums = 0 if sums is None else 5
 
@@ -347,9 +347,9 @@
     column = lambda k, w: (0, k)
     later = lambda k, w: (0, k + skip)
     shapes = [(rows, UNITS)] * 4 + [(2 * rows, 128)]
-    in_specs = [pl.BlockSpec((64, STEP), later if h.shape[1] == D else column) for h in heads]
-    in_specs += [pl.BlockSpec((64 * planes, STEP), column)] * 3
-    in_specs += [pl.BlockSpec((UNITS, STEP), later)] * 4 + [pl.BlockSpec((128, STEP), later)]
+    in_specs = [pl.BlockSpec((64, width), later if h.shape[1] == D else column) for h in heads]
+    in_specs += [pl.BlockSpec((64 * planes, width), column)] * 3
+    in_specs += [pl.BlockSpec((UNITS, width), later)] * 4 + [pl.BlockSpec((128, width), later)]
     args = list(heads) + list(pieces) + list(weights) + [sm] + list(sums or ())
     in_specs += [pl.BlockSpec(s, fixed) for s in shapes[:n_sums]]
     out_shape = [shape(*s, f32) for s in shapes]

time: 159 us -> 158 us (level)
  no operation moved by 1% of the time
where the time goes in v1:
time: 158 us; the launch traced here: 157 us
  starting transfers between devices  55.1 us (35%)
  Pallas kernels  49.1 us (31%)
  waiting for transfers between devices  47.2 us (30%)
  local copies, waits for them, and re-layouts  2.42 us (2%)
  other arithmetic  2.15 us (1%)
    pallas_call x5, Pallas kernels, plane_pass(): pl.pallas_call(kernel, name='plane_pass', grid_spec=pltpu.PrefetchScalarG...  40.3 us
    ppermute x26, starting transfers between devices, move(): return lax.ppermute(a, GROUP, group_pairs(dz, dc, dx))  39.4 us
    ppermute x26, waiting for transfers between devices, move(): return lax.ppermute(a, GROUP, group_pairs(dz, dc, dx))  36.2 us
    ppermute x4, starting transfers between devices, body(): line = lambda d0, d1: lax.ppermute(block, EVERY, z_pairs(d0, d1))  9.66 us
    ppermute x7, waiting for transfers between devices, across(): return lax.ppermute(a, GROUP, opposed_pairs(dz, dx))  5.15 us
    pallas_call x2, Pallas kernels, activate(): pl.pallas_call(kernel, name='activate', grid=(1,), in_specs=[SM] + [pl.Bl...  4.66 us
    pallas_call x14, Pallas kernels, call(): pl.pallas_call(run, name=name, in_specs=list(specs) + [ANY] * (n_dep + n_...  4.17 us
    ppermute x3, waiting for transfers between devices, body(): ckpt = lambda v, d: lax.ppermute(v, ('ckpt',), y_pairs(d))  3.6 us
  transfers between devices with their start and end apart: 40, of which 21 were waited for; matrix products, arithmetic and copies ran while one was open for 0% of the time, Pallas kernels for 27%

profile of v1, /device:TPU:95, one launch (start us, length us, event | category | flops | bytes accessed | tf_op | source)
XLA Modules:
  0.0 157.1 jit_solution(9096453271240425899)
XLA Ops:
  0.0 1.2 select_bitcast_fusion
  1.2 0.8 collective-permute-start
  2.1 0.4 collective-permute-start.11
  2.5 0.7 collective-permute-done.refs_2_
  3.3 0.3 collective-permute-start.4
  3.6 1.3 collective-permute-start.5
  4.9 5.0 %collective-permute-done.1.refs_1_.refs_5_.refs_6_ = bf16[432,5120]{1,0:T(8,128)(2,1)} collective-permute-done((bf16[432,5120]{1,0:T(8,128)(2,1)}, bf16[432,5120]{1,0:T(8,128)(2,1)}, u32[]{:S(2)}, u32[]{:S(2)}) %collective-permute-start.1) | collective-permute-done | bytes 4423712 | tf_op jit(solution)/shard_map/ppermute | solution.py:71
  10.0 4.3 %collective-permute-start.3 = (bf16[64,2560]{1,0:T(8,128)(2,1)S(1)}, bf16[64,2560]{1,0:T(8,128)(2,1)S(1)}, u32[]{:S(2)}, u32[]{:S(2)}) collective-permute-start(bf16[64,2560]{1,0:T(8,128)(2,1)S(1)} %hand.2), channel_id=1, source_target_pairs={{0,8},{1,9},{2,10},{3,11},{4,12},{5,13},{6,14},{7,15},{8,16},{9,17... | collective-permute-start | bytes 983048 | tf_op jit(solution)/shard_map/ppermute | solution.py:71
  14.3 5.0 %collective-permute-done.4.refs_1_.refs_3_ = bf16[64,5120]{1,0:T(8,128)(2,1)S(1)} collective-permute-done((bf16[64,5120]{1,0:T(8,128)(2,1)S(1)}, bf16[64,5120]{1,0:T(8,128)(2,1)S(1)}, u32[]{:S(2)}, u32[]{:S(2)}) %collective-permute-start.4) | collective-permute-done | bytes 655392 | tf_op jit(solution)/shard_map/ppermute | solution.py:71
  19.3 1.1 collective-permute-done.5.refs_2_.refs_1_
  20.4 1.1 pick.7.refs_3_.refs_2_.refs_1_
  21.5 0.8 copy-done
  22.4 1.0 pack.1.refs_11_.refs_17_.refs_16_
  23.4 1.8 %collective-permute-start.12 = (bf16[432,640]{1,0:T(8,128)(2,1)}, bf16[432,640]{1,0:T(8,128)(2,1)}, u32[]{:S(2)}, u32[]{:S(2)}) collective-permute-start(bf16[432,640]{1,0:T(8,128)(2,1)} %pack.1.refs_11_.refs_17_.refs_16_), channel_id=1, source_target_pairs={{0,4},{1,5},{2,6},{3,7},{4,0},{5,1},{6,2},{7,3},{8,12},{9,13},{10,... | collective-permute-start | bytes 1658888 | tf_op jit(solution)/shard_map/ppermute | solution.py:71
  25.2 3.8 %collective-permute-done.2.refs_0_.refs_2_ = bf16[64,2560]{1,0:T(8,128)(2,1)S(1)} collective-permute-done((bf16[64,2560]{1,0:T(8,128)(2,1)S(1)}, bf16[64,2560]{1,0:T(8,128)(2,1)S(1)}, u32[]{:S(2)}, u32[]{:S(2)}) %collective-permute-start.2) | collective-permute-done | bytes 327712 | tf_op jit(solution)/shard_map/ppermute | solution.py:71
  29.1 1.0 regroup.2
  30.4 1.3 collective-permute-start.9
  31.7 1.7 %collective-permute-start.6 = (bf16[64,2560]{1,0:T(8,128)(2,1)}, bf16[64,2560]{1,0:T(8,128)(2,1)S(1)}, u32[]{:S(2)}, u32[]{:S(2)}) collective-permute-start(bf16[64,2560]{1,0:T(8,128)(2,1)} %get-tuple-element.21), channel_id=1, source_target_pairs={{0,8},{1,9},{2,10},{3,11},{4,12},{5,13},{6,14},{7,15},{8,16},{9,17... | collective-permute-start | bytes 983048 | tf_op jit(solution)/shard_map/ppermute | solution.py:71
  33.4 0.7 collective-permute-start.7
  34.0 1.3 copy-done.8
  35.3 0.2 twice.1.refs_5_.refs_8_.refs_9_
  35.6 2.0 %activate.2.refs_6_.refs_9_.refs_15_.refs_14_ = f32[512,432]{1,0:T(8,128)S(1)} custom-call(s32[3]{0:T(128)S(1)} %pad_add_fusion.where, bf16[432,512]{1,0:T(8,128)(2,1)S(1)} %bitcast.48, bf16[432,512]{1,0:T(8,128)(2,1)S(1)} %bitcast.50, bf16[64,5120]{1,0:T(8,128)(2,1)} %pick.7.refs_3_.refs_2_.refs_1_), custom_call_target="tpu_custom_call" | custom-call | tf_op jit(solution)/shard_map/activate/pallas_call | solution.py:229
  37.8 2.6 %activate.3.refs_7_.refs_10_.refs_16_.refs_15_ = f32[512,432]{1,0:T(8,128)S(1)} custom-call(s32[3]{0:T(128)S(1)} %pad_add_fusion.where, bf16[432,640]{1,0:T(8,128)(2,1)} %collective-permute-done.12.refs_0_.refs_12_.refs_18_.refs_17_, bf16[64,5120]{1,0:T(8,128)(2,1)} %pick.7.refs_3_.refs_2_.refs_1_), custom_call_target="tpu_custom_call" | custom-call | tf_op jit(solution)/shard_map/activate/pallas_call | solution.py:229
  40.5 6.7 %collective-permute-done.8.refs_1_.refs_4_ = bf16[128,2560]{1,0:T(8,128)(2,1)S(1)} collective-permute-done((bf16[128,2560]{1,0:T(8,128)(2,1)}, bf16[128,2560]{1,0:T(8,128)(2,1)S(1)}, u32[]{:S(2)}, u32[]{:S(2)}) %collective-permute-start.8) | collective-permute-done | bytes 655392 | tf_op jit(solution)/shard_map/ppermute | solution.py:71
  47.5 1.5 collective-permute-start.15
  49.0 0.4 collective-permute-start.14
  49.6 12.1 %plane_pass.5.refs_3_.refs_18_ = f32[64,128]{1,0:T(8,128)S(1)} custom-call(s32[3]{0:T(128)S(1)} %pad_add_fusion.where, bf16[64,5120]{1,0:T(8,128)(2,1)S(1)} %assemble.1.refs_0_.refs_2_, bf16[64,5120]{1,0:T(8,128)(2,1)S(1)} %copy-done.3, bf16[64,5120]{1,0:T(8,128)(2,1)} %collective-permute-done.10.refs_4_.refs_2_, bf16[64,5120]{1,0:T(8,128)(2,1)S(1)} %copy-done.1, ...), custom_call_target="tpu_custom_call" | custom-call | tf_op jit(solution)/shard_map/plane_pass/pallas_call | solution.py:370
  61.8 0.3 collective-permute-done.15.refs_1_.refs_4_
  62.1 2.8 %collective-permute-done.16.refs_2_ = bf16[128,2560]{1,0:T(8,128)(2,1)S(1)} collective-permute-done((bf16[128,2560]{1,0:T(8,128)(2,1)S(1)}, bf16[128,2560]{1,0:T(8,128)(2,1)S(1)}, u32[]{:S(2)}, u32[]{:S(2)}) %collective-permute-start.16) | collective-permute-done | bytes 655392 | tf_op jit(solution)/shard_map/ppermute | solution.py:71
  65.1 2.1 %collective-permute-start.13 = (bf16[64,2560]{1,0:T(8,128)(2,1)S(1)}, bf16[64,2560]{1,0:T(8,128)(2,1)S(1)}, u32[]{:S(2)}, u32[]{:S(2)}) collective-permute-start(bf16[64,2560]{1,0:T(8,128)(2,1)S(1)} %pick.10.refs_13_), channel_id=1, source_target_pairs={{0,8},{1,9},{2,10},{3,11},{4,28},{5,29},{6,30},{7,31},{8,16},{9,17... | collective-permute-start | bytes 983048 | tf_op jit(solution)/shard_map/ppermute | solution.py:392
  67.2 2.3 %collective-permute-start.21 = (bf16[64,2560]{1,0:T(8,128)(2,1)S(1)}, bf16[64,2560]{1,0:T(8,128)(2,1)S(1)}, u32[]{:S(2)}, u32[]{:S(2)}) collective-permute-start(bf16[64,2560]{1,0:T(8,128)(2,1)S(1)} %collective-permute-done.20.refs_0_), channel_id=1, source_target_pairs={{0,1},{1,2},{2,3},{3,0},{4,5},{5,6},{6,7},{7,4},{8,9},{9,10},{10,1... | collective-permute-start | bytes 983048 | tf_op jit(solution)/shard_map/ppermute | solution.py:71
  69.6 0.2 collective-permute-start.22
  69.8 3.8 %collective-permute-done.14.refs_3_ = bf16[128,2560]{1,0:T(8,128)(2,1)S(1)} collective-permute-done((bf16[128,2560]{1,0:T(8,128)(2,1)S(1)}, bf16[128,2560]{1,0:T(8,128)(2,1)S(1)}, u32[]{:S(2)}, u32[]{:S(2)}) %collective-permute-start.14) | collective-permute-done | bytes 655392 | tf_op jit(solution)/shard_map/ppermute | solution.py:392
  73.7 7.1 %plane_pass.6 = (f32[256,432]{1,0:T(8,128)S(1)}, f32[256,432]{1,0:T(8,128)S(1)}, f32[256,432]{1,0:T(8,128)S(1)}, f32[256,432]{1,0:T(8,128)S(1)}, f32[512,128]{1,0:T(8,128)S(1)}) custom-call(s32[3]{0:T(128)S(1)} %pad_add_fusion.where, bf16[64,2560]{1,0:T(8,128)(2,1)S(1)} %copy-done.10, bf16[64,2560]{1,0:T(8,128)(2,1)S(1)} %copy-done.12, ...), custom_call_target="tpu_custom_call" | custom-call | tf_op jit(solution)/shard_map/plane_pass/pallas_call | solution.py:370
  80.9 2.7 %collective-permute-start.18 = (bf16[64,2560]{1,0:T(8,128)(2,1)S(1)}, bf16[64,2560]{1,0:T(8,128)(2,1)S(1)}, u32[]{:S(2)}, u32[]{:S(2)}) collective-permute-start(bf16[64,2560]{1,0:T(8,128)(2,1)S(1)} %hand.3.refs_3_.refs_0_), channel_id=1, source_target_pairs={{0,1},{1,2},{2,3},{3,0},{4,5},{5,6},{6,7},{7,4},{8,9},{9,10},{10,1... | collective-permute-start | bytes 983048 | tf_op jit(solution)/shard_map/ppermute | solution.py:71
  83.6 4.3 %collective-permute-done.22.refs_2_.refs_1_ = bf16[64,2560]{1,0:T(8,128)(2,1)S(1)} collective-permute-done((bf16[64,2560]{1,0:T(8,128)(2,1)S(1)}, bf16[64,2560]{1,0:T(8,128)(2,1)S(1)}, u32[]{:S(2)}, u32[]{:S(2)}) %collective-permute-start.22) | collective-permute-done | bytes 327712 | tf_op jit(solution)/shard_map/ppermute | solution.py:71
  88.1 8.4 %plane_pass.7.refs_3_.refs_19_ = f32[128,128]{1,0:T(8,128)S(1)} custom-call(s32[3]{0:T(128)S(1)} %pad_add_fusion.where, bf16[64,2560]{1,0:T(8,128)(2,1)S(1)} %collective-permute-done.7.refs_0_.refs_2_, bf16[64,2560]{1,0:T(8,128)(2,1)S(1)} %collective-permute-done.6.refs_1_, bf16[128,2560]{1,0:T(8,128)(2,1)S(1)} %collective-permute-done.16.refs_2_, ...), custom_call_target="tpu_custom_call" | custom-call | tf_op jit(solution)/shard_map/plane_pass/pallas_call | solution.py:370
  96.6 0.3 collective-permute-start.23
  97.0 1.3 collective-permute-done.24.refs_2_
  98.2 6.5 %plane_pass.8 = (f32[128,432]{1,0:T(8,128)S(1)}, f32[128,432]{1,0:T(8,128)S(1)}, f32[128,432]{1,0:T(8,128)S(1)}, f32[128,432]{1,0:T(8,128)S(1)}, f32[256,128]{1,0:T(8,128)S(1)}) custom-call(s32[3]{0:T(128)S(1)} %pad_add_fusion.where, bf16[64,2560]{1,0:T(8,128)(2,1)S(1)} %collective-permute-done.20.refs_0_, ...), custom_call_target="tpu_custom_call" | custom-call | tf_op jit(solution)/shard_map/plane_pass/pallas_call | solution.py:370
  104.8 6.1 %plane_pass.9 = (f32[4,16,128]{2,1,0:T(8,128)S(1)}, f32[4,16,128]{2,1,0:T(8,128)S(1)}, f32[4,16,128]{2,1,0:T(8,128)S(1)}, f32[4,16,128]{2,1,0:T(8,128)S(1)}) custom-call(s32[3]{0:T(128)S(1)} %pad_add_fusion.where, bf16[64,2560]{1,0:T(8,128)(2,1)S(1)} %hand.3.refs_3_.refs_0_, bf16[64,2560]{1,0:T(8,128)(2,1)S(1)} %collective-permute-done.17.refs_2_.refs_1_, ...), custom_call_target="tpu_custom_call" | custom-call | tf_op jit(solution)/shard_map/plane_pass/pallas_call | solution.py:370
  110.9 4.5 %collective-permute-start.25 = (f32[4,16,128]{2,1,0:T(8,128)S(1)}, f32[4,16,128]{2,1,0:T(8,128)S(1)}, u32[]{:S(2)}, u32[]{:S(2)}) collective-permute-start(f32[4,16,128]{2,1,0:T(8,128)S(1)} %get-tuple-element.34), channel_id=1, source_target_pairs={{0,16},{1,17},{2,18},{3,19},{4,20},{5,21},{6,22},{7,23},{8,24},{9,... | collective-permute-start | bytes 98312 | tf_op jit(solution)/shard_map/ppermute | solution.py:71
  115.5 2.4 %collective-permute-start.27 = (f32[4,16,128]{2,1,0:T(8,128)S(1)}, f32[4,16,128]{2,1,0:T(8,128)S(1)}, u32[]{:S(2)}, u32[]{:S(2)}) collective-permute-start(f32[4,16,128]{2,1,0:T(8,128)S(1)} %get-tuple-element.36), channel_id=1, source_target_pairs={{0,24},{1,25},{2,26},{3,27},{4,28},{5,29},{6,30},{7,31},{8,0},{9,1... | collective-permute-start | bytes 98312 | tf_op jit(solution)/shard_map/ppermute | solution.py:71
  117.8 1.6 %collective-permute-done.26 = f32[4,16,128]{2,1,0:T(8,128)S(1)} collective-permute-done((f32[4,16,128]{2,1,0:T(8,128)S(1)}, f32[4,16,128]{2,1,0:T(8,128)S(1)}, u32[]{:S(2)}, u32[]{:S(2)}) %collective-permute-start.26) | collective-permute-done | bytes 32800 | tf_op jit(solution)/shard_map/ppermute | solution.py:71
  119.4 1.2 collective-permute-done.27
  120.6 2.4 %collective-permute-start.28 = (f32[4,16,128]{2,1,0:T(8,128)S(1)}, f32[4,16,128]{2,1,0:T(8,128)S(1)}, u32[]{:S(2)}, u32[]{:S(2)}) collective-permute-start(f32[4,16,128]{2,1,0:T(8,128)S(1)} %add_add_fusion.1), channel_id=1, source_target_pairs={{0,2},{1,3},{2,0},{3,1},{4,6},{5,7},{6,4},{7,5},{8,10},{9,11},{10,... | collective-permute-start | bytes 98312 | tf_op jit(solution)/shard_map/ppermute | solution.py:71
  123.0 1.5 collective-permute-start.30
  124.5 0.5 collective-permute-done.28
  125.0 0.8 collective-permute-done.29
  125.8 1.2 collective-permute-done.30
  127.0 7.7 %collective-permute-start.31 = (f32[4,16,128]{2,1,0:T(8,128)S(1)}, f32[4,16,128]{2,1,0:T(8,128)S(1)}, u32[]{:S(2)}, u32[]{:S(2)}) collective-permute-start(f32[4,16,128]{2,1,0:T(8,128)S(1)} %add_add_fusion), channel_id=1, source_target_pairs={{0,4},{1,5},{2,6},{3,7},{4,0},{5,1},{6,2},{7,3},{8,12},{9,13},{10,... | collective-permute-start | bytes 98312 | tf_op jit(solution)/shard_map/ppermute | solution.py:71
  135.4 0.2 collective-permute-done.31
  135.9 1.0 collective-permute-start.32
  136.8 1.9 %collective-permute-start.33 = (f32[1,4]{1,0:T(1,128)S(1)}, f32[1,4]{1,0:T(1,128)S(1)}, u32[]{:S(2)}, u32[]{:S(2)}) collective-permute-start(f32[1,4]{1,0:T(1,128)S(1)} %dynamic-slice_bitcast_fusion), channel_id=1, source_target_pairs={{0,32},{32,64},{64,96},{96,0},{128,160},{160,192},{192,224},{224,1... | collective-permute-start | bytes 56 | tf_op jit(solution)/shard_map/ppermute | solution.py:501
  138.7 1.0 collective-permute-done.32
  139.8 2.6 %collective-permute-done.34 = f32[1,4]{1,0:T(1,128)S(1)} collective-permute-done((f32[1,4]{1,0:T(1,128)S(1)}, f32[1,4]{1,0:T(1,128)S(1)}, u32[]{:S(2)}, u32[]{:S(2)}) %collective-permute-start.34) | collective-permute-done | bytes 48 | tf_op jit(solution)/shard_map/ppermute | solution.py:501
  142.4 3.3 %collective-permute-start.35 = (f32[1,4]{1,0:T(1,128)S(1)}, f32[1,4]{1,0:T(1,128)S(1)}, u32[]{:S(2)}, u32[]{:S(2)}) collective-permute-start(f32[1,4]{1,0:T(1,128)S(1)} %add_add_fusion.2), channel_id=1, source_target_pairs={{0,16},{1,17},{2,18},{3,19},{4,132},{5,133},{6,134},{7,135},{32,48... | collective-permute-start | bytes 56 | tf_op jit(solution)/shard_map/ppermute | solution.py:503
  145.7 0.8 collective-permute-start.36
  146.5 3.6 %collective-permute-start.37 = (f32[1,4]{1,0:T(1,128)S(1)}, f32[1,4]{1,0:T(1,128)S(1)}, u32[]{:S(2)}, u32[]{:S(2)}) collective-permute-start(f32[1,4]{1,0:T(1,128)S(1)} %add_add_fusion.2), channel_id=1, source_target_pairs={{0,24},{1,25},{2,26},{3,27},{4,140},{5,141},{6,142},{7,143},{32,56... | collective-permute-start | bytes 56 | tf_op jit(solution)/shard_map/ppermute | solution.py:503
  150.2 1.9 %collective-permute-start.38 = (f32[1,4]{1,0:T(1,128)S(1)}, f32[1,4]{1,0:T(1,128)S(1)}, u32[]{:S(2)}, u32[]{:S(2)}) collective-permute-start(f32[1,4]{1,0:T(1,128)S(1)} %add_add_fusion.2), channel_id=1, source_target_pairs={{4,156},{5,157},{6,158},{7,159},{36,188},{37,189},{38,190},{39,191... | collective-permute-start | bytes 56 | tf_op jit(solution)/shard_map/ppermute | solution.py:503
  152.1 2.3 %collective-permute-done.38 = f32[1,4]{1,0:T(1,128)S(1)} collective-permute-done((f32[1,4]{1,0:T(1,128)S(1)}, f32[1,4]{1,0:T(1,128)S(1)}, u32[]{:S(2)}, u32[]{:S(2)}) %collective-permute-start.38) | collective-permute-done | bytes 48 | tf_op jit(solution)/shard_map/ppermute | solution.py:503
  154.4 1.4 collective-permute-start.39
  155.8 0.8 collective-permute-done.39
  156.6 0.5 add.80
  (89 shorter events, 2.4 us)
Async XLA Ops:
  1.2 2.0 %collective-permute-start = (bf16[32,5120]{1,0:T(8,128)(2,1)S(1)}, bf16[32,5120]{1,0:T(8,128)(2,1)S(1)}, u32[]{:S(2)}, u32[]{:S(2)}) collective-permute-start(bf16[32,5120]{1,0:T(8,128)(2,1)S(1)} %pad_maximum_fusion.1), channel_id=1, source_target_pairs={{0,4},{1,5},{2,6},{3,7},{4,0},{5,1},{6,2},{7,3},{8,12},{9,13},{10,... | collective-permute-start | bytes 983048 | tf_op jit(solution)/shard_map/ppermute | solution.py:71
  2.0 7.9 %collective-permute-start.1 = (bf16[432,5120]{1,0:T(8,128)(2,1)}, bf16[432,5120]{1,0:T(8,128)(2,1)}, u32[]{:S(2)}, u32[]{:S(2)}) collective-permute-start(bf16[432,5120]{1,0:T(8,128)(2,1)} %bitcast.31), channel_id=1, source_target_pairs={{0,4},{1,5},{2,6},{3,7},{4,0},{5,1},{6,2},{7,3},{8,12},{9,13},{10,... | collective-permute-start | bytes 13271048 | tf_op jit(solution)/shard_map/ppermute | solution.py:71
  2.1 20.3 %collective-permute-start.11 = (bf16[432,5120]{1,0:T(8,128)(2,1)}, bf16[432,5120]{1,0:T(8,128)(2,1)}, u32[]{:S(2)}, u32[]{:S(2)}) collective-permute-start(bf16[432,5120]{1,0:T(8,128)(2,1)} %bitcast.39), channel_id=1, source_target_pairs={{0,4},{1,5},{2,6},{3,7},{4,0},{5,1},{6,2},{7,3},{8,12},{9,13},{10,... | collective-permute-start | bytes 13271048 | tf_op jit(solution)/shard_map/ppermute | solution.py:71
  3.3 19.1 %copy-start.4 = (bf16[1,512,432]{1,2,0:T(8,128)(2,1)S(1)}, bf16[1,512,432]{1,2,0:T(8,128)(2,1)}, u32[]{:S(2)}) copy-start(bf16[1,512,432]{1,2,0:T(8,128)(2,1)} %param.15) | copy-start | bytes 1327108
  3.3 19.1 %copy-start.6 = (bf16[1,512,432]{1,2,0:T(8,128)(2,1)S(1)}, bf16[1,512,432]{1,2,0:T(8,128)(2,1)}, u32[]{:S(2)}) copy-start(bf16[1,512,432]{1,2,0:T(8,128)(2,1)} %param.16) | copy-start | bytes 1327108
  3.3 19.1 %copy-start.13 = (s32[432,64]{0,1:T(8,128)S(1)}, s32[432,64]{0,1:T(8,128)}, u32[]{:S(2)}) copy-start(s32[432,64]{0,1:T(8,128)} %param.19) | copy-start | bytes 331780
  3.3 16.0 %collective-permute-start.4 = (bf16[64,5120]{1,0:T(8,128)(2,1)S(1)}, bf16[64,5120]{1,0:T(8,128)(2,1)S(1)}, u32[]{:S(2)}, u32[]{:S(2)}) collective-permute-start(bf16[64,5120]{1,0:T(8,128)(2,1)S(1)} %assemble.1.refs_0_.refs_2_), channel_id=1, source_target_pairs={{0,1},{1,2},{2,3},{3,0},{4,5},{5,6},{6,7},{7,4},{8,9},{9,10},{10,1... | collective-permute-start | bytes 1966088 | tf_op jit(solution)/shard_map/ppermute | solution.py:71
  3.6 16.8 %collective-permute-start.5 = (bf16[64,5120]{1,0:T(8,128)(2,1)S(1)}, bf16[64,5120]{1,0:T(8,128)(2,1)S(1)}, u32[]{:S(2)}, u32[]{:S(2)}) collective-permute-start(bf16[64,5120]{1,0:T(8,128)(2,1)S(1)} %assemble.1.refs_0_.refs_2_), channel_id=1, source_target_pairs={{0,3},{1,0},{2,1},{3,2},{4,7},{5,4},{6,5},{7,6},{8,11},{9,8},{10,9... | collective-permute-start | bytes 1966088 | tf_op jit(solution)/shard_map/ppermute | solution.py:71
  9.9 19.1 %collective-permute-start.2 = (bf16[64,2560]{1,0:T(8,128)(2,1)S(1)}, bf16[64,2560]{1,0:T(8,128)(2,1)S(1)}, u32[]{:S(2)}, u32[]{:S(2)}) collective-permute-start(bf16[64,2560]{1,0:T(8,128)(2,1)S(1)} %hand.2), channel_id=1, source_target_pairs={{0,24},{1,25},{2,26},{3,27},{4,28},{5,29},{6,30},{7,31},{8,0},{9,1... | collective-permute-start | bytes 983048 | tf_op jit(solution)/shard_map/ppermute | solution.py:71
  10.0 19.0 %collective-permute-start.3 = (bf16[64,2560]{1,0:T(8,128)(2,1)S(1)}, bf16[64,2560]{1,0:T(8,128)(2,1)S(1)}, u32[]{:S(2)}, u32[]{:S(2)}) collective-permute-start(bf16[64,2560]{1,0:T(8,128)(2,1)S(1)} %hand.2), channel_id=1, source_target_pairs={{0,8},{1,9},{2,10},{3,11},{4,12},{5,13},{6,14},{7,15},{8,16},{9,17... | collective-permute-start | bytes 983048 | tf_op jit(solution)/shard_map/ppermute | solution.py:71
  20.4 9.6 %copy-start.2 = (bf16[64,5120]{1,0:T(8,128)(2,1)}, bf16[64,5120]{1,0:T(8,128)(2,1)S(1)}, u32[]{:S(2)}) copy-start(bf16[64,5120]{1,0:T(8,128)(2,1)S(1)} %collective-permute-done.5.refs_2_.refs_1_) | copy-start | bytes 1966084
  21.5 0.8 copy-start
  22.3 18.2 %collective-permute-start.10 = (bf16[64,5120]{1,0:T(8,128)(2,1)}, bf16[64,5120]{1,0:T(8,128)(2,1)}, u32[]{:S(2)}, u32[]{:S(2)}) collective-permute-start(bf16[64,5120]{1,0:T(8,128)(2,1)} %pick.7.refs_3_.refs_2_.refs_1_), channel_id=1, source_target_pairs={{0,1},{1,2},{2,3},{3,0},{4,7},{5,4},{6,5},{7,6},{8,9},{9,10},{10,1... | collective-permute-start | bytes 1966088 | tf_op jit(solution)/shard_map/ppermute | solution.py:392
  23.4 9.9 %collective-permute-start.12 = (bf16[432,640]{1,0:T(8,128)(2,1)}, bf16[432,640]{1,0:T(8,128)(2,1)}, u32[]{:S(2)}, u32[]{:S(2)}) collective-permute-start(bf16[432,640]{1,0:T(8,128)(2,1)} %pack.1.refs_11_.refs_17_.refs_16_), channel_id=1, source_target_pairs={{0,4},{1,5},{2,6},{3,7},{4,0},{5,1},{6,2},{7,3},{8,12},{9,13},{10,... | collective-permute-start | bytes 1658888 | tf_op jit(solution)/shard_map/ppermute | solution.py:71
  29.0 1.1 copy-start.9
  29.0 1.1 copy-start.11
  29.0 6.6 %copy-start.5 = (bf16[1,512,432]{1,2,0:T(8,128)(2,1)S(1)}, bf16[1,512,432]{1,2,0:T(8,128)(2,1)}, u32[]{:S(2)}) copy-start(bf16[1,512,432]{1,2,0:T(8,128)(2,1)} %param.15) | copy-start | bytes 1327108
  29.0 6.6 %copy-start.7 = (bf16[1,512,432]{1,2,0:T(8,128)(2,1)S(1)}, bf16[1,512,432]{1,2,0:T(8,128)(2,1)}, u32[]{:S(2)}) copy-start(bf16[1,512,432]{1,2,0:T(8,128)(2,1)} %param.16) | copy-start | bytes 1327108
  30.2 17.0 %collective-permute-start.8 = (bf16[128,2560]{1,0:T(8,128)(2,1)}, bf16[128,2560]{1,0:T(8,128)(2,1)S(1)}, u32[]{:S(2)}, u32[]{:S(2)}) collective-permute-start(bf16[128,2560]{1,0:T(8,128)(2,1)} %get-tuple-element.22.refs_3_), channel_id=1, source_target_pairs={{0,1},{1,2},{2,3},{3,0},{4,5},{5,6},{6,7},{7,4},{8,9},{9,10},{10,1... | collective-permute-start | bytes 1966088 | tf_op jit(solution)/shard_map/ppermute | solution.py:71
  30.4 16.8 %collective-permute-start.9 = (bf16[128,2560]{1,0:T(8,128)(2,1)}, bf16[128,2560]{1,0:T(8,128)(2,1)S(1)}, u32[]{:S(2)}, u32[]{:S(2)}) collective-permute-start(bf16[128,2560]{1,0:T(8,128)(2,1)} %get-tuple-element.22.refs_3_), channel_id=1, source_target_pairs={{0,3},{1,0},{2,1},{3,2},{4,7},{5,4},{6,5},{7,6},{8,11},{9,8},{10,9... | collective-permute-start | bytes 1966088 | tf_op jit(solution)/shard_map/ppermute | solution.py:71
  31.7 15.8 %collective-permute-start.6 = (bf16[64,2560]{1,0:T(8,128)(2,1)}, bf16[64,2560]{1,0:T(8,128)(2,1)S(1)}, u32[]{:S(2)}, u32[]{:S(2)}) collective-permute-start(bf16[64,2560]{1,0:T(8,128)(2,1)} %get-tuple-element.21), channel_id=1, source_target_pairs={{0,8},{1,9},{2,10},{3,11},{4,12},{5,13},{6,14},{7,15},{8,16},{9,17... | collective-permute-start | bytes 983048 | tf_op jit(solution)/shard_map/ppermute | solution.py:71
  33.4 14.1 %collective-permute-start.7 = (bf16[64,2560]{1,0:T(8,128)(2,1)}, bf16[64,2560]{1,0:T(8,128)(2,1)S(1)}, u32[]{:S(2)}, u32[]{:S(2)}) collective-permute-start(bf16[64,2560]{1,0:T(8,128)(2,1)} %get-tuple-element.21), channel_id=1, source_target_pairs={{0,24},{1,25},{2,26},{3,27},{4,28},{5,29},{6,30},{7,31},{8,0},{9,1... | collective-permute-start | bytes 983048 | tf_op jit(solution)/shard_map/ppermute | solution.py:71
  34.0 1.3 copy-start.8
  35.3 2.3 %copy-start.10 = (bf16[64,2560]{1,0:T(8,128)(2,1)S(1)}, bf16[64,2560]{1,0:T(8,128)(2,1)}, u32[]{:S(2)}) copy-start(bf16[64,2560]{1,0:T(8,128)(2,1)} %copy-done.9) | copy-start | bytes 983044
  35.3 2.3 %copy-start.12 = (bf16[64,2560]{1,0:T(8,128)(2,1)S(1)}, bf16[64,2560]{1,0:T(8,128)(2,1)}, u32[]{:S(2)}) copy-start(bf16[64,2560]{1,0:T(8,128)(2,1)} %copy-done.11) | copy-start | bytes 983044
  37.7 11.9 %slice-start.2 = ((s8[4423680]{0:T(1024)(128)(4,1)}), s8[4194304]{0:T(1024)(128)(4,1)S(1)}, s32[]{:S(2)}) async-start(s8[4423680]{0:T(1024)(128)(4,1)} %bitcast.40), calls=%async_computation.2 | async-start | bytes 8388608
  37.8 11.8 %slice-start = ((s8[4423680]{0:T(1024)(128)(4,1)}), s8[4194304]{0:T(1024)(128)(4,1)S(1)}, s32[]{:S(2)}) async-start(s8[4423680]{0:T(1024)(128)(4,1)} %bitcast.32), calls=%async_computation | async-start | bytes 8388608
  40.5 9.1 %slice-start.1 = ((s8[4423680]{0:T(1024)(128)(4,1)}), s8[229376]{0:T(1024)(128)(4,1)S(1)}, s32[]{:S(2)}) async-start(s8[4423680]{0:T(1024)(128)(4,1)} %bitcast.32), calls=%async_computation.1 | async-start | bytes 458752
  40.5 9.1 %slice-start.3 = ((s8[4423680]{0:T(1024)(128)(4,1)}), s8[229376]{0:T(1024)(128)(4,1)S(1)}, s32[]{:S(2)}) async-start(s8[4423680]{0:T(1024)(128)(4,1)} %bitcast.40), calls=%async_computation.3 | async-start | bytes 458752
  40.5 9.1 %copy-start.1 = (bf16[64,5120]{1,0:T(8,128)(2,1)S(1)}, bf16[64,5120]{1,0:T(8,128)(2,1)}, u32[]{:S(2)}) copy-start(bf16[64,5120]{1,0:T(8,128)(2,1)} %copy-done) | copy-start | bytes 1966084
  40.5 9.1 %copy-start.3 = (bf16[64,5120]{1,0:T(8,128)(2,1)S(1)}, bf16[64,5120]{1,0:T(8,128)(2,1)}, u32[]{:S(2)}) copy-start(bf16[64,5120]{1,0:T(8,128)(2,1)} %copy-done.2) | copy-start | bytes 1966084
  47.5 14.6 %collective-permute-start.15 = (bf16[128,2560]{1,0:T(8,128)(2,1)S(1)}, bf16[128,2560]{1,0:T(8,128)(2,1)S(1)}, u32[]{:S(2)}, u32[]{:S(2)}) collective-permute-start(bf16[128,2560]{1,0:T(8,128)(2,1)S(1)} %regroup.3.refs_3_), channel_id=1, source_target_pairs={{0,1},{1,2},{2,3},{3,0},{4,5},{5,6},{6,7},{7,4},{8,9},{9,10},{10,1... | collective-permute-start | bytes 1966088 | tf_op jit(solution)/shard_map/ppermute | solution.py:71
  49.0 15.8 %collective-permute-start.16 = (bf16[128,2560]{1,0:T(8,128)(2,1)S(1)}, bf16[128,2560]{1,0:T(8,128)(2,1)S(1)}, u32[]{:S(2)}, u32[]{:S(2)}) collective-permute-start(bf16[128,2560]{1,0:T(8,128)(2,1)S(1)} %regroup.3.refs_3_), channel_id=1, source_target_pairs={{0,3},{1,0},{2,1},{3,2},{4,7},{5,4},{6,5},{7,6},{8,11},{9,8},{10,9... | collective-permute-start | bytes 1966088 | tf_op jit(solution)/shard_map/ppermute | solution.py:71
  49.0 24.6 %collective-permute-start.14 = (bf16[128,2560]{1,0:T(8,128)(2,1)S(1)}, bf16[128,2560]{1,0:T(8,128)(2,1)S(1)}, u32[]{:S(2)}, u32[]{:S(2)}) collective-permute-start(bf16[128,2560]{1,0:T(8,128)(2,1)S(1)} %pick.9.refs_2_), channel_id=1, source_target_pairs={{0,1},{1,2},{2,3},{3,0},{4,7},{5,4},{6,5},{7,6},{8,9},{9,10},{10,1... | collective-permute-start | bytes 1966088 | tf_op jit(solution)/shard_map/ppermute | solution.py:392
  49.5 17.8 %collective-permute-start.20 = (bf16[64,2560]{1,0:T(8,128)(2,1)S(1)}, bf16[64,2560]{1,0:T(8,128)(2,1)S(1)}, u32[]{:S(2)}, u32[]{:S(2)}) collective-permute-start(bf16[64,2560]{1,0:T(8,128)(2,1)S(1)} %pick.8.refs_3_), channel_id=1, source_target_pairs={{0,8},{1,9},{2,10},{3,11},{4,28},{5,29},{6,30},{7,31},{8,16},{9,17... | collective-permute-start | bytes 983048 | tf_op jit(solution)/shard_map/ppermute | solution.py:392
  65.0 23.1 %collective-permute-start.19 = (bf16[128,2560]{1,0:T(8,128)(2,1)S(1)}, bf16[128,2560]{1,0:T(8,128)(2,1)S(1)}, u32[]{:S(2)}, u32[]{:S(2)}) collective-permute-start(bf16[128,2560]{1,0:T(8,128)(2,1)S(1)} %pick.11.refs_10_), channel_id=1, source_target_pairs={{0,1},{1,2},{2,3},{3,0},{4,7},{5,4},{6,5},{7,6},{8,9},{9,10},{10,1... | collective-permute-start | bytes 1966088 | tf_op jit(solution)/shard_map/ppermute | solution.py:392
  65.1 15.7 %collective-permute-start.13 = (bf16[64,2560]{1,0:T(8,128)(2,1)S(1)}, bf16[64,2560]{1,0:T(8,128)(2,1)S(1)}, u32[]{:S(2)}, u32[]{:S(2)}) collective-permute-start(bf16[64,2560]{1,0:T(8,128)(2,1)S(1)} %pick.10.refs_13_), channel_id=1, source_target_pairs={{0,8},{1,9},{2,10},{3,11},{4,28},{5,29},{6,30},{7,31},{8,16},{9,17... | collective-permute-start | bytes 983048 | tf_op jit(solution)/shard_map/ppermute | solution.py:392
  67.2 16.4 %collective-permute-start.21 = (bf16[64,2560]{1,0:T(8,128)(2,1)S(1)}, bf16[64,2560]{1,0:T(8,128)(2,1)S(1)}, u32[]{:S(2)}, u32[]{:S(2)}) collective-permute-start(bf16[64,2560]{1,0:T(8,128)(2,1)S(1)} %collective-permute-done.20.refs_0_), channel_id=1, source_target_pairs={{0,1},{1,2},{2,3},{3,0},{4,5},{5,6},{6,7},{7,4},{8,9},{9,10},{10,1... | collective-permute-start | bytes 983048 | tf_op jit(solution)/shard_map/ppermute | solution.py:71
  69.6 18.4 %collective-permute-start.22 = (bf16[64,2560]{1,0:T(8,128)(2,1)S(1)}, bf16[64,2560]{1,0:T(8,128)(2,1)S(1)}, u32[]{:S(2)}, u32[]{:S(2)}) collective-permute-start(bf16[64,2560]{1,0:T(8,128)(2,1)S(1)} %collective-permute-done.20.refs_0_), channel_id=1, source_target_pairs={{0,3},{1,0},{2,1},{3,2},{4,7},{5,4},{6,5},{7,6},{8,11},{9,8},{10,9... | collective-permute-start | bytes 983048 | tf_op jit(solution)/shard_map/ppermute | solution.py:71
  80.8 15.7 %collective-permute-start.17 = (bf16[64,2560]{1,0:T(8,128)(2,1)S(1)}, bf16[64,2560]{1,0:T(8,128)(2,1)S(1)}, u32[]{:S(2)}, u32[]{:S(2)}) collective-permute-start(bf16[64,2560]{1,0:T(8,128)(2,1)S(1)} %hand.3.refs_3_.refs_0_), channel_id=1, source_target_pairs={{0,3},{1,0},{2,1},{3,2},{4,7},{5,4},{6,5},{7,6},{8,11},{9,8},{10,9... | collective-permute-start | bytes 983048 | tf_op jit(solution)/shard_map/ppermute | solution.py:71
  80.9 15.6 %collective-permute-start.18 = (bf16[64,2560]{1,0:T(8,128)(2,1)S(1)}, bf16[64,2560]{1,0:T(8,128)(2,1)S(1)}, u32[]{:S(2)}, u32[]{:S(2)}) collective-permute-start(bf16[64,2560]{1,0:T(8,128)(2,1)S(1)} %hand.3.refs_3_.refs_0_), channel_id=1, source_target_pairs={{0,1},{1,2},{2,3},{3,0},{4,5},{5,6},{6,7},{7,4},{8,9},{9,10},{10,1... | collective-permute-start | bytes 983048 | tf_op jit(solution)/shard_map/ppermute | solution.py:71
  88.0 10.2 %collective-permute-start.24 = (bf16[64,2560]{1,0:T(8,128)(2,1)S(1)}, bf16[64,2560]{1,0:T(8,128)(2,1)S(1)}, u32[]{:S(2)}, u32[]{:S(2)}) collective-permute-start(bf16[64,2560]{1,0:T(8,128)(2,1)S(1)} %pick.12.refs_19_), channel_id=1, source_target_pairs={{0,1},{1,2},{2,3},{3,0},{4,7},{5,4},{6,5},{7,6},{8,9},{9,10},{10,1... | collective-permute-start | bytes 983048 | tf_op jit(solution)/shard_map/ppermute | solution.py:392
  96.6 8.1 %collective-permute-start.23 = (bf16[64,2560]{1,0:T(8,128)(2,1)S(1)}, bf16[64,2560]{1,0:T(8,128)(2,1)S(1)}, u32[]{:S(2)}, u32[]{:S(2)}) collective-permute-start(bf16[64,2560]{1,0:T(8,128)(2,1)S(1)} %pick.13.refs_9_), channel_id=1, source_target_pairs={{0,1},{1,2},{2,3},{3,0},{4,7},{5,4},{6,5},{7,6},{8,9},{9,10},{10,1... | collective-permute-start | bytes 983048 | tf_op jit(solution)/shard_map/ppermute | solution.py:392
  110.9 6.9 %collective-permute-start.25 = (f32[4,16,128]{2,1,0:T(8,128)S(1)}, f32[4,16,128]{2,1,0:T(8,128)S(1)}, u32[]{:S(2)}, u32[]{:S(2)}) collective-permute-start(f32[4,16,128]{2,1,0:T(8,128)S(1)} %get-tuple-element.34), channel_id=1, source_target_pairs={{0,16},{1,17},{2,18},{3,19},{4,20},{5,21},{6,22},{7,23},{8,24},{9,... | collective-permute-start | bytes 98312 | tf_op jit(solution)/shard_map/ppermute | solution.py:71
  115.5 4.0 %collective-permute-start.26 = (f32[4,16,128]{2,1,0:T(8,128)S(1)}, f32[4,16,128]{2,1,0:T(8,128)S(1)}, u32[]{:S(2)}, u32[]{:S(2)}) collective-permute-start(f32[4,16,128]{2,1,0:T(8,128)S(1)} %get-tuple-element.35), channel_id=1, source_target_pairs={{0,8},{1,9},{2,10},{3,11},{4,12},{5,13},{6,14},{7,15},{8,16},{9,17... | collective-permute-start | bytes 98312 | tf_op jit(solution)/shard_map/ppermute | solution.py:71
  115.5 5.2 %collective-permute-start.27 = (f32[4,16,128]{2,1,0:T(8,128)S(1)}, f32[4,16,128]{2,1,0:T(8,128)S(1)}, u32[]{:S(2)}, u32[]{:S(2)}) collective-permute-start(f32[4,16,128]{2,1,0:T(8,128)S(1)} %get-tuple-element.36), channel_id=1, source_target_pairs={{0,24},{1,25},{2,26},{3,27},{4,28},{5,29},{6,30},{7,31},{8,0},{9,1... | collective-permute-start | bytes 98312 | tf_op jit(solution)/shard_map/ppermute | solution.py:71
  120.6 4.4 %collective-permute-start.28 = (f32[4,16,128]{2,1,0:T(8,128)S(1)}, f32[4,16,128]{2,1,0:T(8,128)S(1)}, u32[]{:S(2)}, u32[]{:S(2)}) collective-permute-start(f32[4,16,128]{2,1,0:T(8,128)S(1)} %add_add_fusion.1), channel_id=1, source_target_pairs={{0,2},{1,3},{2,0},{3,1},{4,6},{5,7},{6,4},{7,5},{8,10},{9,11},{10,... | collective-permute-start | bytes 98312 | tf_op jit(solution)/shard_map/ppermute | solution.py:71
  123.0 2.8 %collective-permute-start.29 = (f32[4,16,128]{2,1,0:T(8,128)S(1)}, f32[4,16,128]{2,1,0:T(8,128)S(1)}, u32[]{:S(2)}, u32[]{:S(2)}) collective-permute-start(f32[4,16,128]{2,1,0:T(8,128)S(1)} %add_add_fusion.1), channel_id=1, source_target_pairs={{0,1},{1,2},{2,3},{3,0},{4,5},{5,6},{6,7},{7,4},{8,9},{9,10},{10,1... | collective-permute-start | bytes 98312 | tf_op jit(solution)/shard_map/ppermute | solution.py:71
  123.0 4.0 %collective-permute-start.30 = (f32[4,16,128]{2,1,0:T(8,128)S(1)}, f32[4,16,128]{2,1,0:T(8,128)S(1)}, u32[]{:S(2)}, u32[]{:S(2)}) collective-permute-start(f32[4,16,128]{2,1,0:T(8,128)S(1)} %add_add_fusion.1), channel_id=1, source_target_pairs={{0,3},{1,0},{2,1},{3,2},{4,7},{5,4},{6,5},{7,6},{8,11},{9,8},{10,9... | collective-permute-start | bytes 98312 | tf_op jit(solution)/shard_map/ppermute | solution.py:71
  127.0 8.6 %collective-permute-start.31 = (f32[4,16,128]{2,1,0:T(8,128)S(1)}, f32[4,16,128]{2,1,0:T(8,128)S(1)}, u32[]{:S(2)}, u32[]{:S(2)}) collective-permute-start(f32[4,16,128]{2,1,0:T(8,128)S(1)} %add_add_fusion), channel_id=1, source_target_pairs={{0,4},{1,5},{2,6},{3,7},{4,0},{5,1},{6,2},{7,3},{8,12},{9,13},{10,... | collective-permute-start | bytes 98312 | tf_op jit(solution)/shard_map/ppermute | solution.py:71
  135.9 3.9 %collective-permute-start.32 = (f32[1,4]{1,0:T(1,128)S(1)}, f32[1,4]{1,0:T(1,128)S(1)}, u32[]{:S(2)}, u32[]{:S(2)}) collective-permute-start(f32[1,4]{1,0:T(1,128)S(1)} %dynamic-slice_bitcast_fusion), channel_id=1, source_target_pairs={{0,64},{32,96},{64,0},{96,32},{128,192},{160,224},{192,128},{224,1... | collective-permute-start | bytes 56 | tf_op jit(solution)/shard_map/ppermute | solution.py:501
  136.8 2.9 %collective-permute-start.33 = (f32[1,4]{1,0:T(1,128)S(1)}, f32[1,4]{1,0:T(1,128)S(1)}, u32[]{:S(2)}, u32[]{:S(2)}) collective-permute-start(f32[1,4]{1,0:T(1,128)S(1)} %dynamic-slice_bitcast_fusion), channel_id=1, source_target_pairs={{0,32},{32,64},{64,96},{96,0},{128,160},{160,192},{192,224},{224,1... | collective-permute-start | bytes 56 | tf_op jit(solution)/shard_map/ppermute | solution.py:501
  138.7 3.6 %collective-permute-start.34 = (f32[1,4]{1,0:T(1,128)S(1)}, f32[1,4]{1,0:T(1,128)S(1)}, u32[]{:S(2)}, u32[]{:S(2)}) collective-permute-start(f32[1,4]{1,0:T(1,128)S(1)} %dynamic-slice_bitcast_fusion), channel_id=1, source_target_pairs={{0,96},{32,0},{64,32},{96,64},{128,224},{160,128},{192,160},{224,1... | collective-permute-start | bytes 56 | tf_op jit(solution)/shard_map/ppermute | solution.py:501
  142.4 9.7 %collective-permute-start.35 = (f32[1,4]{1,0:T(1,128)S(1)}, f32[1,4]{1,0:T(1,128)S(1)}, u32[]{:S(2)}, u32[]{:S(2)}) collective-permute-start(f32[1,4]{1,0:T(1,128)S(1)} %add_add_fusion.2), channel_id=1, source_target_pairs={{0,16},{1,17},{2,18},{3,19},{4,132},{5,133},{6,134},{7,135},{32,48... | collective-permute-start | bytes 56 | tf_op jit(solution)/shard_map/ppermute | solution.py:503
  145.7 6.4 %collective-permute-start.36 = (f32[1,4]{1,0:T(1,128)S(1)}, f32[1,4]{1,0:T(1,128)S(1)}, u32[]{:S(2)}, u32[]{:S(2)}) collective-permute-start(f32[1,4]{1,0:T(1,128)S(1)} %add_add_fusion.2), channel_id=1, source_target_pairs={{0,8},{1,9},{2,10},{3,11},{4,148},{5,149},{6,150},{7,151},{32,40},... | collective-permute-start | bytes 56 | tf_op jit(solution)/shard_map/ppermute | solution.py:503
  146.5 5.6 %collective-permute-start.37 = (f32[1,4]{1,0:T(1,128)S(1)}, f32[1,4]{1,0:T(1,128)S(1)}, u32[]{:S(2)}, u32[]{:S(2)}) collective-permute-start(f32[1,4]{1,0:T(1,128)S(1)} %add_add_fusion.2), channel_id=1, source_target_pairs={{0,24},{1,25},{2,26},{3,27},{4,140},{5,141},{6,142},{7,143},{32,56... | collective-permute-start | bytes 56 | tf_op jit(solution)/shard_map/ppermute | solution.py:503
  150.2 4.3 %collective-permute-start.38 = (f32[1,4]{1,0:T(1,128)S(1)}, f32[1,4]{1,0:T(1,128)S(1)}, u32[]{:S(2)}, u32[]{:S(2)}) collective-permute-start(f32[1,4]{1,0:T(1,128)S(1)} %add_add_fusion.2), channel_id=1, source_target_pairs={{4,156},{5,157},{6,158},{7,159},{36,188},{37,189},{38,190},{39,191... | collective-permute-start | bytes 56 | tf_op jit(solution)/shard_map/ppermute | solution.py:503
  154.4 2.2 %collective-permute-start.39 = (f32[1,4]{1,0:T(1,128)S(1)}, f32[1,4]{1,0:T(1,128)S(1)}, u32[]{:S(2)}, u32[]{:S(2)}) collective-permute-start(f32[1,4]{1,0:T(1,128)S(1)} %broadcast_select_fusion), channel_id=1, source_target_pairs={{0,4},{1,5},{2,6},{3,7},{4,0},{5,1},{6,2},{7,3},{8,12},{9,13},{10,... | collective-permute-start | bytes 56 | tf_op jit(solution)/shard_map/ppermute | solution.py:71
